TPU v7x, 512 devices: a whole 4x8x8 slice. The times are simulated.
512 devices in a mesh: dp: 32 (over y_hi, z), fsdp: 16 (over x, y_lo, core).
Axes of the slice: x: 4, y: 8 (y_hi: 4, y_lo: 2; y = y_hi * 2 + y_lo), z: 8, core: 2. Of those that a mesh axis runs over, the one named last changes fastest.
Arguments:
- queries: bfloat16 [16, 256, 4096], P('fsdp', 'dp'), may hold values from -0.125 to 0.125
- passages: bfloat16 [16, 256, 4096], P('fsdp', 'dp'), may hold values from -0.125 to 0.125
- positives: int32 [16, 256], P('fsdp', 'dp'), may hold values from 0 to 255, each once within a row
- hard_blocks: int32 [16, 256], P('fsdp', 'dp'), may hold values from 0 to 63
- residual: bfloat16 [16, 4096, 4096], P('fsdp', 'dp'), may hold values from -6 to 6
- hidden_act: bfloat16 [16, 4096, 14336], P('fsdp', 'dp'), may hold values from -6 to 6
- gain: bfloat16 [4096], replicated, may hold values from 0.099609375 to 1.8984375
- down_rows: bfloat16 [16, 14336], P(None, 'fsdp'), may hold values from -0.046875 to 0.046875
- up_weight_rows: bfloat16 [16, 4096], P(None, 'fsdp'), may hold values from -0.09375 to 0.09375
Outputs:
- query_grads: bfloat16 [16, 256, 4096], P('fsdp', 'dp')
- passage_grads: bfloat16 [16, 256, 4096], P('fsdp', 'dp')
- grad_down: float32 [16, 14336], P(None, 'fsdp')
- grad_up: float32 [16, 4096], P(None, 'fsdp')
Inputs may be any that keep to these rules, and one draw needn't show every extreme that they name: `positives`: within each group every passage is the positive of exactly one query.
All inputs are finite; a program needn't handle non-finite values.
Results may differ from a plain program's by a relative error of at most 0.02.
Values may be sent and summed in bfloat16 or wider, within the bound.
A program may use at most 64 MiB of HBM per device.

v0:
```python
import jax
import jax.numpy as jnp
from jax import lax
from jax.sharding import PartitionSpec as P

HB = 4


inverse_warmth_factor = 50.0
difficult_distractor_extra = 1.3862943611198906
lowrank_scale = 2.0
norm_eps = 1e-06


def unit_rows(values):
    floats = values.astype(jnp.float32)
    length = jnp.sqrt(jnp.sum(floats * floats, axis=-1, keepdims=True) + norm_eps)
    return (floats / length, length)


def tangent(unit_vec, gradient, length):
    return (gradient - unit_vec * jnp.sum(unit_vec * gradient, axis=-1, keepdims=True)) / length


def product_along_first(first_op, second_op):
    return lax.dot_general(
        first_op, second_op, (((0,), (0,)), ((), ())), preferred_element_type=jnp.float32
    )


def product_along_second(first_op, second_op):
    return lax.dot_general(
        first_op, second_op, (((1,), (1,)), ((), ())), preferred_element_type=jnp.float32
    )


def adapter_terms(residual_sequence, hidden_seq, upstream, gain, down_full, complete_up_weight):
    seq_len = residual_sequence.shape[0]
    reduced_values = product_along_second(hidden_seq, down_full).astype(jnp.bfloat16)
    residual_flow = residual_sequence.astype(jnp.float32) + lowrank_scale * jnp.dot(
        reduced_values, complete_up_weight, preferred_element_type=jnp.float32
    )
    root_mean = jnp.sqrt(jnp.mean(residual_flow * residual_flow, axis=-1, keepdims=True) + norm_eps)
    normed = residual_flow / root_mean
    grad_norm = gain.astype(jnp.float32)[None, :] * upstream[None, :] / seq_len
    residual_flow_gradient = (
        (grad_norm - normed * jnp.mean(grad_norm * normed, axis=-1, keepdims=True)) / root_mean
    ).astype(jnp.bfloat16)
    up_weight_term = lowrank_scale * product_along_first(reduced_values, residual_flow_gradient)
    reduced_gradient = (
        lowrank_scale * product_along_second(residual_flow_gradient, complete_up_weight)
    ).astype(jnp.bfloat16)
    term_down = product_along_first(reduced_gradient, hidden_seq)
    return (term_down, up_weight_term)


def per_device(
    queries, passages, positives, hard_blocks, residual, hidden_act, gain, down_rows, up_weight_rows
):
    unit_query, len_query = unit_rows(queries[0])
    unit_passage, len_passage = unit_rows(passages[0])
    question_vector = unit_query.astype(jnp.bfloat16)
    document_vector = unit_passage.astype(jnp.bfloat16)
    query_count = question_vector.shape[0]
    own_count = document_vector.shape[0]
    feature = question_vector.shape[1]
    data_size = lax.axis_size("dp")
    down_full, complete_up_weight = (
        lax.all_gather(down_rows, "fsdp", axis=1, tiled=True),
        lax.all_gather(up_weight_rows, "fsdp", axis=1, tiled=True),
    )
    cluster_documents = lax.all_gather(document_vector, "dp", axis=0, tiled=True)
    passage_ids = lax.iota(jnp.int32, cluster_documents.shape[0])
    cosine_matrix = inverse_warmth_factor * product_along_second(question_vector, cluster_documents)
    difficult_distractor_indicator = (passage_ids[None, :] // HB == hard_blocks[0][:, None]).astype(
        jnp.float32
    )
    normalized_probabilities = jnp.exp(
        cosine_matrix + difficult_distractor_extra * difficult_distractor_indicator
    )
    softmax_rows = normalized_probabilities / jnp.sum(
        normalized_probabilities, axis=1, keepdims=True
    )
    target = (passage_ids[None, :] == positives[0][:, None]).astype(jnp.float32)
    multiplier_factors = (softmax_rows - target).astype(jnp.bfloat16)
    factor_along_axis = multiplier_factors.reshape(query_count, data_size, own_count)
    passage_block_list = cluster_documents.reshape(data_size, own_count, feature)
    question_share = inverse_warmth_factor * jnp.einsum(
        "akh,khb->kab", factor_along_axis, passage_block_list, preferred_element_type=jnp.float32
    )
    query_raw = jnp.sum(question_share.astype(jnp.bfloat16).astype(jnp.float32), axis=0)
    incomplete_amount = (
        (inverse_warmth_factor * product_along_first(multiplier_factors, question_vector))
        .astype(jnp.bfloat16)
        .astype(jnp.float32)
    )
    passage_raw = lax.psum_scatter(
        incomplete_amount.astype(jnp.bfloat16), "dp", scatter_dimension=0, tiled=True
    ).astype(jnp.float32)
    query_full = tangent(unit_query, query_raw, len_query)
    passage_full = tangent(unit_passage, passage_raw, len_passage)
    term_down, up_weight_term = adapter_terms(
        residual[0], hidden_act[0], query_full[0], gain, down_full, complete_up_weight
    )
    total_down, total_up = lax.psum((term_down, up_weight_term), ("dp", "fsdp"))
    owner_index = lax.axis_index("fsdp")
    down_width = down_rows.shape[1]
    up_width = up_weight_rows.shape[1]
    grad_down = lax.dynamic_slice_in_dim(total_down, owner_index * down_width, down_width, 1)
    grad_up = lax.dynamic_slice_in_dim(total_up, owner_index * up_width, up_width, 1)
    query_grads = query_full.astype(jnp.bfloat16)[None]
    passage_grads = passage_full.astype(jnp.bfloat16)[None]
    return (query_grads, passage_grads, grad_down, grad_up)


def solution(mesh):
    in_specs = (
        P("fsdp", "dp", None),
        P("fsdp", "dp", None),
        P("fsdp", "dp"),
        P("fsdp", "dp"),
        P("fsdp", "dp", None),
        P("fsdp", "dp", None),
        P(),
        P(None, "fsdp"),
        P(None, "fsdp"),
    )
    out_specs = (P("fsdp", "dp", None), P("fsdp", "dp", None), P(None, "fsdp"), P(None, "fsdp"))
    return jax.shard_map(
        per_device, mesh=mesh, in_specs=in_specs, out_specs=out_specs, check_vma=False
    )
```

profile of v0, /device:TPU:2, one launch (start us, length us, event | category | flops | bytes accessed | tf_op | source)
XLA Modules:
  0.0 621.7 jit_solution(14570908845083764187)
XLA Ops:
  7.2 1.0 fusion.27
  8.2 1.6 fusion.36
  9.8 0.7 broadcast_in_dim.10
  10.5 19.9 %all_gather.11 = bf16[16,4096]{1,0:T(8,128)(2,1)S(1)} all-gather(bf16[16,256]{1,0:T(8,128)(2,1)} %param.17), channel_id=1, replica_groups=mesh['dp'=32,'fsdp'=16] {'fsdp'}, dimensions={1}, use_global_device_ids=true | all-gather | bytes 139264 | tf_op jit(solution)/shard_map/all_gather | solution.py:70
  30.4 1.0 fusion.23
  31.4 20.4 %all_gather.10 = bf16[16,14336]{1,0:T(8,128)(2,1)S(1)} all-gather(bf16[16,896]{1,0:T(8,128)(2,1)} %param.16), channel_id=1, replica_groups=mesh['dp'=32,'fsdp'=16] {'fsdp'}, dimensions={1}, use_global_device_ids=true | all-gather | bytes 487424 | tf_op jit(solution)/shard_map/all_gather | solution.py:69
  51.8 3.2 fusion.15
  55.1 0.6 multiply_reduce_fusion.1
  55.7 46.9 %all-gather.2.cloned.1.call-done = bf16[256,4096]{1,0:T(8,128)(2,1)} async-done(((bf16[8,4096]{1,0:T(8,128)(2,1)}), bf16[256,4096]{1,0:T(8,128)(2,1)}) %all-gather.2.cloned.1.call-update) | async-done | bytes 2097168 | tf_op jit(solution)/shard_map/all_gather | solution.py:72
  102.5 2.4 fusion.39
  105.1 2.3 fusion.9
  107.4 0.2 fusion.18
  107.7 0.4 multiply_reduce_fusion
  108.1 0.4 divide_convert_fusion
  108.5 4.5 fusion.4
  113.0 0.9 convolution_multiply_fusion.3
  114.1 2.1 fusion.2
  116.2 0.7 fusion.28
  116.9 266.5 %all-reduce.3.cloned.1.call-done = (f32[16,14336]{1,0:T(8,128)}, f32[16,4096]{1,0:T(8,128)}) async-done(((f32[16,14336]{1,0:T(8,128)}, f32[16,4096]{1,0:T(8,128)}), (f32[16,14336]{1,0:T(8,128)}, f32[16,4096]{1,0:T(8,128)})) %all-reduce.3.cloned.1.call-update) | async-done | bytes 1179664 | tf_op jit(solution)/shard_map/psum | solution.py:105
  383.4 1.3 constant_dynamic-slice_fusion
  384.7 1.4 constant_dynamic-slice_fusion.1
  386.2 226.4 %reduce-scatter.2.cloned.1.call-done = bf16[8,4096]{1,0:T(8,128)(2,1)} async-done(((bf16[256,4096]{1,0:T(8,128)(2,1)}), bf16[8,4096]{1,0:T(8,128)(2,1)}) %reduce-scatter.2.cloned.1.call-update) | async-done | bytes 65552 | tf_op jit(solution)/shard_map/reduce_scatter | solution.py:97
  612.5 1.1 fusion.20
  613.6 1.6 fusion.30
  (24 shorter events, 0.5 us)
Async XLA Ops:
  7.2 95.4 %all-gather.2.cloned.1.call-start = ((), (), s32[]{:S(2)}) async-start(), calls=%async_computation.1 | async-start | bytes 2162688 | tf_op jit(solution)/shard_map/all_gather | solution.py:72
  9.8 373.6 %all-reduce.3.cloned.1.call-start = ((), (), s32[]{:S(2)}) async-start(), calls=%async_computation.3 | async-start | bytes 2359296 | tf_op jit(solution)/shard_map/psum | solution.py:105
  51.8 3.2 copy-start.2
  55.0 47.5 %copy-start = (bf16[1,8,4096]{2,1,0:T(8,128)(2,1)S(1)}, bf16[1,8,4096]{2,1,0:T(8,128)(2,1)}, u32[]{:S(2)}) copy-start(bf16[1,8,4096]{2,1,0:T(8,128)(2,1)} %param.9) | copy-start | bytes 196612
  55.0 47.5 %copy-start.4 = (s32[1,8]{1,0:T(1,128)S(1)}, s32[1,8]{1,0:T(1,128)}, u32[]{:S(2)}) copy-start(s32[1,8]{1,0:T(1,128)} %param.12) | copy-start | bytes 100
  55.0 49.9 %copy-start.3 = (s32[1,8]{1,0:T(1,128)S(1)}, s32[1,8]{1,0:T(1,128)}, u32[]{:S(2)}) copy-start(s32[1,8]{1,0:T(1,128)} %param.11) | copy-start | bytes 100
  114.0 498.5 %copy-start.1 = (bf16[1,8,4096]{2,1,0:T(8,128)(2,1)S(1)}, bf16[1,8,4096]{2,1,0:T(8,128)(2,1)}, u32[]{:S(2)}) copy-start(bf16[1,8,4096]{2,1,0:T(8,128)(2,1)} %param.10) | copy-start | bytes 196612
  114.0 498.5 %reduce-scatter.2.cloned.1.call-start = ((), (), s32[]{:S(2)}) async-start(), calls=%async_computation.2 | async-start | bytes 2162688 | tf_op jit(solution)/shard_map/reduce_scatter | solution.py:97
Sparse Core Ops, SparseCore 0:
  11.7 90.7 all-gather.1
  114.1 269.2 all-reduce.2
  388.5 224.0 reduce-scatter.1
where the time goes:
time: 622 us
  waiting for transfers between devices  540 us (87%)
  blocking collectives  40.3 us (6%)
  matrix products  16 us (3%)
  between operations  13.8 us (2%)
  other arithmetic  8.78 us (1%)
    psum x1, waiting for transfers between devices, per_device(): total_down, total_up = lax.psum((term_down, up_weight_term), ('dp', 'fsdp'))  266 us
    reduce_scatter x1, waiting for transfers between devices, per_device(): lax.psum_scatter(incomplete_amount.astype(jnp.bfloat16), 'dp', scatter_di...  226 us
    all_gather x1, waiting for transfers between devices, per_device(): lax.all_gather(document_vector, 'dp', axis=0, tiled=True)  46.9 us
    all_gather x1, blocking collectives, per_device(): lax.all_gather(down_rows, 'fsdp', axis=1, tiled=True)  20.4 us
    all_gather x1, blocking collectives, per_device(): lax.all_gather(up_weight_rows, 'fsdp', axis=1, tiled=True)  19.9 us
  transfers between devices with their start and end apart: 3, of which 3 were waited for; matrix products, arithmetic and copies ran while one was open for 2% of the time, Pallas kernels for 0%

commit v1 on v0

v1 whole, which is shorter than its diff:
```python
import functools

import jax
import jax.numpy as jnp
from jax import lax
from jax.experimental import pallas as pl
from jax.experimental.pallas import tpu as pltpu
from jax.sharding import PartitionSpec as P

HB = 4
NZ = 8
SCALE = 50.0
EXTRA = 1.3862943611198906
EPS = 1e-06
F32 = jnp.float32
BF16 = jnp.bfloat16
MESH = pl.DeviceIdType.MESH


def dot(a, b, ca=1, cb=0):
    return lax.dot_general(a, b, (((ca,), (cb,)), ((), ())), preferred_element_type=F32)


def landed(ref, sem):
    pltpu.make_async_copy(ref, ref, sem).wait()


def loop(low, high, body):
    def step(k, carry):
        body(k)
        return carry

    lax.fori_loop(low, high, step, 0)


def as_column(row):
    n = row.shape[1]
    wide = jnp.broadcast_to(row, (n, n))
    eye = lax.broadcasted_iota(jnp.int32, (n, n), 0) == lax.broadcasted_iota(jnp.int32, (n, n), 1)
    return jnp.sum(jnp.where(eye, wide, 0.0), axis=1, keepdims=True)


def as_row(column):
    n = column.shape[0]
    wide = jnp.broadcast_to(column, (n, n))
    eye = lax.broadcasted_iota(jnp.int32, (n, n), 0) == lax.broadcasted_iota(jnp.int32, (n, n), 1)
    return jnp.sum(jnp.where(eye, wide, 0.0), axis=0, keepdims=True)


def split_rows(ref):
    wide = ref[...].astype(F32)
    n, _, w = wide.shape
    return [wide[:, 8 * h : 8 * h + 8, :].reshape(8 * n, w).astype(BF16) for h in (0, 1)]


def stacked(block):
    half = block.shape[-1] // 2
    return jnp.concatenate([block[:, :half], block[:, half:]], axis=0)


def kernel(
    ndp, nf,
    q_in, p_in, pos_in, hard_in, gain_in, down_in, up_in, res_hbm, hid_hbm,
    qg_out, pg_out, gd_out, gu_out,
    hid, res, normed, unit_q, unit_p, gain_row,
    eq, ep, rq, rp, pmat, qmat, ps, rs, rc, qs, rqr, pgs, rpg,
    rw, upf, sm, rmate, sa, ra, tiles, rb, rt,
    sem, msem, asem,
):
    nz = NZ
    ni = nf // 2
    rank, dw = down_in.shape
    uw = up_in.shape[1]
    sw = dw + uw
    d_model = unit_q.shape[1]
    fb = d_model // nz
    hw = fb // 2
    seq = res.shape[0]
    pg = ndp * 8
    n_tiles = tiles.shape[0]
    nc = sw // 128

    d = lax.axis_index("dp")
    f = lax.axis_index("fsdp")
    y, z = lax.div(d, nz), lax.rem(d, nz)
    i0, core = lax.div(f, 2), lax.rem(f, 2)
    mate = (d, 2 * i0 + 1 - core)

    def at_z(tz):
        return (y * nz + tz, f)

    def at_i(i):
        return (d, 2 * i + core)

    def send(src, dst, send_sem, recv_sem, device):
        pltpu.make_async_remote_copy(
            src_ref=src, dst_ref=dst, send_sem=send_sem, recv_sem=recv_sem,
            device_id=device, device_id_type=MESH,
        ).start()

    load_hid = pltpu.make_async_copy(hid_hbm.at[0], hid, sem.at[0])
    load_res = pltpu.make_async_copy(res_hbm.at[0], res, sem.at[1])
    load_hid.start()
    load_res.start()

    barrier = pltpu.get_barrier_semaphore()

    def greet(device):
        pl.semaphore_signal(barrier, inc=1, device_id=device, device_id_type=MESH)

    loop(1, ndp, lambda k: greet((lax.rem(d + k, ndp), f)))
    loop(1, ni, lambda k: greet(at_i(lax.rem(i0 + k, ni))))
    greet(mate)

    def unit_rows(ref, unit_ref, blocks):
        rows = ref[0].astype(F32)
        length = jnp.sqrt(jnp.sum(rows * rows, axis=1, keepdims=True) + EPS)
        unit = rows / length
        unit_ref[...] = unit
        for k in range(nz):
            blocks[k] = stacked(unit[:, k * fb : (k + 1) * fb]).astype(BF16)
        return length

    len_p = unit_rows(p_in, unit_p, ep)
    len_q = unit_rows(q_in, unit_q, eq)
    rp[d] = ep[z]
    rq[z] = eq[z]
    rw[core, i0] = jnp.concatenate([down_in[...], up_in[...]], axis=1)

    pl.semaphore_wait(barrier, (ndp - 1) + (ni - 1) + 1)

    def send_p(k):
        t = lax.rem(d + k, ndp)
        send(ep.at[lax.rem(t, nz)], rp.at[d], sem.at[2], sem.at[3], (t, f))

    def send_q(k):
        tz = lax.rem(z + k, nz)
        send(eq.at[tz], rq.at[z], sem.at[4], sem.at[5], at_z(tz))

    def send_w(k):
        i = lax.rem(i0 + k, ni)
        send(rw.at[core, i0], rw.at[core, i0], sem.at[6], sem.at[7], at_i(i))

    loop(1, ndp, send_p)
    loop(1, nz, send_q)
    loop(1, ni, send_w)

    for k in range(gain_in.shape[0]):
        gain_row[0:1, 128 * k : 128 * (k + 1)] = gain_in[...].astype(F32)[k : k + 1, :]

    landed(rq.at[pl.ds(0, nz - 1)], sem.at[5])
    landed(rp.at[pl.ds(0, ndp - 1)], sem.at[3])
    for h, half in enumerate(split_rows(rp)):
        pmat[h] = half
    for h, half in enumerate(split_rows(rq)):
        qmat[h] = half
    partial = dot(qmat[0], pmat[0], 1, 1) + dot(qmat[1], pmat[1], 1, 1)
    ps[...] = partial.reshape(nz, 8, pg)
    rs[z] = ps[z]

    def send_s(k):
        tz = lax.rem(z + k, nz)
        send(ps.at[tz], rs.at[z], sem.at[8], sem.at[9], at_z(tz))

    loop(1, nz, send_s)

    landed(rw.at[core, pl.ds(0, ni - 1)], sem.at[7])
    send(rw.at[core], rw.at[core], sem.at[10], sem.at[11], mate)
    load_hid.wait()

    def reduce_part(c, start):
        def step(i, acc):
            cols = pl.ds(pl.multiple_of((2 * i + c) * dw, 128), dw)
            return acc + dot(rw[c, i][:, :dw], hid[:, cols], 1, 1)

        return lax.fori_loop(0, ni, step, start)

    reduced_t = reduce_part(core, jnp.zeros((rank, seq), F32))

    landed(rs.at[pl.ds(0, nz - 1)], sem.at[9])
    ids = lax.broadcasted_iota(jnp.int32, (8, pg), 1)
    pos = as_column(pos_in[...].astype(F32))
    hard = as_column(hard_in[...].astype(F32))
    blocks = lax.shift_right_logical(ids, 2).astype(F32)
    logits = SCALE * jnp.sum(rs[...], axis=0) + jnp.where(blocks == hard, EXTRA, 0.0)
    weights = jnp.exp(logits)
    soft = weights / jnp.sum(weights, axis=1, keepdims=True)
    coeffs = soft - jnp.where(ids.astype(F32) == pos, 1.0, 0.0)
    rc[z] = stacked(coeffs).astype(BF16)

    def send_c(k):
        send(rc.at[z], rc.at[z], sem.at[12], sem.at[13], at_z(lax.rem(z + k, nz)))

    loop(1, nz, send_c)

    landed(rw.at[1 - core], sem.at[11])
    reduced_t = reduce_part(1 - core, reduced_t).astype(BF16)
    for c in range(2):
        for i in range(ni):
            at = (2 * i + c) * uw
            upf[:, at : at + uw] = rw[c, i][:, dw:]

    landed(rc.at[pl.ds(0, nz - 1)], sem.at[13])
    cmat = jnp.concatenate(split_rows(rc), axis=1)
    for h in range(2):
        qs[:, :, h * hw : (h + 1) * hw] = (SCALE * dot(cmat, pmat[h])).reshape(nz, 8, hw)
    rqr[z] = qs[z]

    def send_qr(k):
        tz = lax.rem(z + k, nz)
        send(qs.at[tz], rqr.at[z], sem.at[14], sem.at[15], at_z(tz))

    loop(1, nz, send_qr)
    terms = [(SCALE * dot(cmat, qmat[h], 0, 0)).reshape(ndp, 8, hw) for h in range(2)]
    pgs[...] = jnp.concatenate(terms, axis=1).astype(BF16)
    rpg[d] = pgs[d]

    def send_pg(k):
        t = lax.rem(d + k, ndp)
        send(pgs.at[t], rpg.at[d], sem.at[16], sem.at[17], (t, f))

    loop(1, ndp, send_pg)

    load_res.wait()
    cw = 512 if d_model % 512 == 0 else 128
    reduced = reduced_t.astype(F32).T.astype(BF16)

    def forward(j, squares):
        cols = pl.ds(pl.multiple_of(j * cw, 128), cw)
        part = res[:, cols].astype(F32) + 2.0 * dot(reduced, upf[:, cols])
        normed[:, cols] = part
        return squares + jnp.sum(part * part, axis=1, keepdims=True)

    squares = lax.fori_loop(0, d_model // cw, forward, jnp.zeros((seq, 1), F32))
    inv_root = 1.0 / jnp.sqrt(squares / d_model + EPS)
    inv_row = as_row(inv_root)

    def normalize(j, acc):
        cols = pl.ds(pl.multiple_of(j * cw, 128), cw)
        part = normed[:, cols] * inv_root
        normed[:, cols] = part
        high = part.astype(BF16)
        low = (part - high.astype(F32)).astype(BF16)
        return acc + (dot(upf[:, cols], high, 1, 1) + dot(upf[:, cols], low, 1, 1))

    normed_up = lax.fori_loop(0, d_model // cw, normalize, jnp.zeros((rank, seq), F32))

    landed(rqr.at[pl.ds(0, nz - 1)], sem.at[15])

    def tangent(unit_ref, pieces, length, out_ref):
        raw = jnp.concatenate(pieces, axis=1)
        unit = unit_ref[...]
        full = (raw - unit * jnp.sum(unit * raw, axis=1, keepdims=True)) / length
        out_ref[0] = full.astype(BF16)
        return full

    query_full = tangent(unit_q, [rqr[k] for k in range(nz)], len_q, qg_out)

    grad_norm = gain_row[...] * query_full[0:1, :] * (1.0 / seq)
    projected = jnp.sum(normed[...] * grad_norm, axis=1, keepdims=True) * (1.0 / d_model)
    up_grad = jnp.sum(upf[...].astype(F32) * grad_norm, axis=1, keepdims=True)
    grad_reduced_t = (2.0 * (up_grad - as_row(projected) * normed_up) * inv_row).astype(BF16)

    def terms_of(i, c):
        owner = 2 * i + c
        down_cols = pl.ds(pl.multiple_of(owner * dw, 128), dw)
        up_cols = pl.ds(pl.multiple_of(owner * uw, 128), uw)
        down_term = dot(grad_reduced_t, hid[:, down_cols])
        stream = ((gn[:, up_cols] - normed[:, up_cols] * projected) * inv_root).astype(BF16)
        return down_term, 2.0 * dot(reduced_t, stream)

    gn = gain_row
    gn[...] = grad_norm

    def for_mate(i):
        down_term, up_term = terms_of(i, 1 - core)
        sm[i, :, :dw] = down_term.astype(BF16)
        sm[i, :, dw:] = up_term.astype(BF16)
        send(sm.at[i], rmate.at[i], sem.at[18], msem.at[i], mate)

    def mate_step(k):
        for_mate(lax.rem(i0 + k, ni))

    loop(1, ni + 1, mate_step)

    def own_terms(i, out_ref, out_at):
        down_term, up_term = terms_of(i, core)
        landed(rmate.at[i], msem.at[i])
        other = rmate[i].astype(F32)
        out_ref[out_at, :, :dw] = (down_term + other[:, :dw]).astype(BF16)
        out_ref[out_at, :, dw:] = (up_term + other[:, dw:]).astype(BF16)

    def own_step(k):
        i = lax.rem(i0 + k, ni)
        own_terms(i, sa, i)
        send(sa.at[i], ra.at[i0], sem.at[19], sem.at[20], at_i(i))

    loop(1, ni, own_step)
    own_terms(i0, ra, i0)

    landed(ra.at[pl.ds(0, ni - 1)], sem.at[20])
    total = jnp.sum(ra[...].astype(F32), axis=0)
    for k in range(n_tiles):
        h, c = k // nc, k % nc
        tiles[k] = total[8 * h : 8 * h + 8, 128 * c : 128 * c + 128]

    own_tile = lax.div(d * n_tiles + ndp - 1, ndp)
    is_owner = (lax.div(own_tile * ndp, n_tiles) == d) & (own_tile < n_tiles)

    def send_tile(k):
        t = lax.div(k * ndp, n_tiles)

        @pl.when(t != d)
        def _():
            send(tiles.at[k], rb.at[d], sem.at[21], sem.at[22], (t, f))

    loop(0, n_tiles, send_tile)

    landed(rpg.at[pl.ds(0, ndp - 1)], sem.at[17])
    pieces = []
    for k in range(nz):
        both = rpg[k].astype(F32)
        for a in range(1, ndp // nz):
            both = both + rpg[a * nz + k].astype(F32)
        pieces += [both[:8], both[8:]]
    tangent(unit_p, pieces, len_p, pg_out)

    @pl.when(is_owner)
    def _():
        rb[d] = tiles[own_tile]
        landed(rb.at[pl.ds(0, ndp - 1)], sem.at[22])
        rt[own_tile] = jnp.sum(rb[...], axis=0)

        def send_total(k):
            t = lax.rem(d + k, ndp)
            send(rt.at[own_tile], rt.at[own_tile], sem.at[23], sem.at[24], (t, f))

        loop(1, ndp, send_total)
        landed(rt.at[pl.ds(0, n_tiles - 1)], sem.at[24])

    @pl.when(jnp.logical_not(is_owner))
    def _():
        landed(rt, sem.at[24])

    for k in range(n_tiles):
        h, c = k // nc, k % nc
        if c < dw // 128:
            gd_out[8 * h : 8 * h + 8, 128 * c : 128 * c + 128] = rt[k]
        else:
            at = 128 * c - dw
            gu_out[8 * h : 8 * h + 8, at : at + 128] = rt[k]

    landed(rp.at[pl.ds(0, ndp - 1)], sem.at[2])
    landed(rq.at[pl.ds(0, nz - 1)], sem.at[4])
    landed(rw.at[0, pl.ds(0, ni - 1)], sem.at[6])
    landed(rs.at[pl.ds(0, nz - 1)], sem.at[8])
    landed(rw.at[0], sem.at[10])
    landed(rc.at[pl.ds(0, nz - 1)], sem.at[12])
    landed(rqr.at[pl.ds(0, nz - 1)], sem.at[14])
    landed(rpg.at[pl.ds(0, ndp - 1)], sem.at[16])
    landed(sm, sem.at[18])
    landed(sa.at[pl.ds(0, ni - 1)], sem.at[19])

    @pl.when(is_owner)
    def _():
        landed(tiles.at[pl.ds(0, n_tiles - 1)], sem.at[21])
        landed(rb.at[pl.ds(0, ndp - 1)], sem.at[23])

    @pl.when(jnp.logical_not(is_owner))
    def _():
        landed(tiles, sem.at[21])


def per_device(ndp, nf, queries, passages, positives, hard_blocks, residual, hidden_act, gain, down_rows, up_rows):
    d_model = queries.shape[2]
    seq, hid = hidden_act.shape[1:]
    rank, dw = down_rows.shape
    uw = up_rows.shape[1]
    sw = dw + uw
    ni = nf // 2
    fb = d_model // NZ
    hw = fb // 2
    pg = ndp * 8
    n_tiles = (rank // 8) * (sw // 128)
    vmem = pl.BlockSpec(memory_space=pltpu.VMEM)
    anywhere = pl.BlockSpec(memory_space=pl.ANY)
    return pl.pallas_call(
        functools.partial(kernel, ndp, nf),
        out_shape=(
            jax.ShapeDtypeStruct(queries.shape, BF16),
            jax.ShapeDtypeStruct(passages.shape, BF16),
            jax.ShapeDtypeStruct(down_rows.shape, F32),
            jax.ShapeDtypeStruct(up_rows.shape, F32),
        ),
        in_specs=[vmem] * 7 + [anywhere] * 2,
        out_specs=(vmem,) * 4,
        scratch_shapes=[
            pltpu.VMEM((seq, hid), BF16),
            pltpu.VMEM((seq, d_model), BF16),
            pltpu.VMEM((seq, d_model), F32),
            pltpu.VMEM((8, d_model), F32),
            pltpu.VMEM((8, d_model), F32),
            pltpu.VMEM((1, d_model), F32),
            pltpu.VMEM((NZ, 16, hw), BF16),
            pltpu.VMEM((NZ, 16, hw), BF16),
            pltpu.VMEM((NZ, 16, hw), BF16),
            pltpu.VMEM((ndp, 16, hw), BF16),
            pltpu.VMEM((2, pg, hw), BF16),
            pltpu.VMEM((2, 8 * NZ, hw), BF16),
            pltpu.VMEM((NZ, 8, pg), F32),
            pltpu.VMEM((NZ, 8, pg), F32),
            pltpu.VMEM((NZ, 16, pg // 2), BF16),
            pltpu.VMEM((NZ, 8, fb), F32),
            pltpu.VMEM((NZ, 8, fb), F32),
            pltpu.VMEM((ndp, 16, hw), BF16),
            pltpu.VMEM((ndp, 16, hw), BF16),
            pltpu.VMEM((2, ni, rank, sw), BF16),
            pltpu.VMEM((rank, d_model), BF16),
            pltpu.VMEM((ni, rank, sw), BF16),
            pltpu.VMEM((ni, rank, sw), BF16),
            pltpu.VMEM((ni, rank, sw), BF16),
            pltpu.VMEM((ni, rank, sw), BF16),
            pltpu.VMEM((n_tiles, 8, 128), F32),
            pltpu.VMEM((ndp, 8, 128), F32),
            pltpu.VMEM((n_tiles, 8, 128), F32),
            pltpu.SemaphoreType.DMA((25,)),
            pltpu.SemaphoreType.DMA((ni,)),
            pltpu.SemaphoreType.DMA((1,)),
        ],
        compiler_params=pltpu.CompilerParams(
            collective_id=0, has_side_effects=True, vmem_limit_bytes=40 * 1024 * 1024
        ),
        name="contrastive_adapter",
    )(
        queries, passages, positives, hard_blocks, gain.reshape(d_model // 128, 128),
        down_rows, up_rows, residual, hidden_act,
    )


def solution(mesh):
    wide = P("fsdp", "dp", None)
    in_specs = (
        wide, wide, P("fsdp", "dp"), P("fsdp", "dp"), wide, wide, P(), P(None, "fsdp"), P(None, "fsdp"),
    )
    out_specs = (wide, wide, P(None, "fsdp"), P(None, "fsdp"))
    body = functools.partial(per_device, mesh.shape["dp"], mesh.shape["fsdp"])
    return jax.shard_map(body, mesh=mesh, in_specs=in_specs, out_specs=out_specs, check_vma=False)
```

time: 622 us -> 80.2 us (0.13)
  the two profiles are of different devices: /device:TPU:2 before, /device:TPU:4 now
where the time goes in v1:
time: 80.2 us; the launch traced here: 79.8 us
  Pallas kernels  68.2 us (85%)
  local copies, waits for them, and re-layouts  10.9 us (14%)
    pallas_call x1, Pallas kernels, per_device(): pl.pallas_call(functools.partial(kernel, ndp, nf), out_shape=(jax.ShapeDt...  68.2 us
    unnamed x22, local copies, waits for them, and re-layouts  10.9 us

profile of v1, /device:TPU:4, one launch (start us, length us, event | category | flops | bytes accessed | tf_op | source)
XLA Modules:
  0.0 79.8 jit_solution(1906420672492654003)
XLA Ops:
  0.6 0.0 copy-start
  0.6 2.0 %copy-done = bf16[1,128,14336]{2,1,0:T(8,128)(2,1)S(1)} copy-done((bf16[1,128,14336]{2,1,0:T(8,128)(2,1)S(1)}, bf16[1,128,14336]{2,1,0:T(8,128)(2,1)}, u32[]{:S(2)}) %copy-start) | copy-done | bytes 3670040
  2.7 0.0 copy-start.1
  2.7 1.2 %copy-done.1 = bf16[1,128,4096]{2,1,0:T(8,128)(2,1)S(1)} copy-done((bf16[1,128,4096]{2,1,0:T(8,128)(2,1)S(1)}, bf16[1,128,4096]{2,1,0:T(8,128)(2,1)}, u32[]{:S(2)}) %copy-start.1) | copy-done | bytes 1048600
  3.9 0.0 copy-start.2
  3.9 0.8 %copy-done.2 = bf16[1,8,4096]{2,1,0:T(8,128)(2,1)S(1)} copy-done((bf16[1,8,4096]{2,1,0:T(8,128)(2,1)S(1)}, bf16[1,8,4096]{2,1,0:T(8,128)(2,1)}, u32[]{:S(2)}) %copy-start.2) | copy-done | bytes 65560
  4.7 0.0 copy-start.3
  4.7 0.8 %copy-done.3 = bf16[1,8,4096]{2,1,0:T(8,128)(2,1)S(1)} copy-done((bf16[1,8,4096]{2,1,0:T(8,128)(2,1)S(1)}, bf16[1,8,4096]{2,1,0:T(8,128)(2,1)}, u32[]{:S(2)}) %copy-start.3) | copy-done | bytes 65560
  5.6 0.0 copy-start.4
  5.6 0.7 copy-done.4
  6.3 0.0 copy-start.5
  6.3 0.7 copy-done.5
  7.0 0.0 copy-start.6
  7.0 0.7 copy-done.6
  7.7 0.0 copy-start.7
  7.7 0.7 copy-done.7
  8.4 0.0 copy-start.8
  8.4 0.7 copy-done.8
  9.0 68.2 %contrastive_adapter.1 = (bf16[1,8,4096]{2,1,0:T(8,128)(2,1)S(1)}, bf16[1,8,4096]{2,1,0:T(8,128)(2,1)S(1)}, f32[16,896]{1,0:T(8,128)S(1)}, f32[16,256]{1,0:T(8,128)S(1)}) custom-call(bf16[1,8,4096]{2,1,0:T(8,128)(2,1)S(1)} %copy-done.2, bf16[1,8,4096]{2,1,0:T(8,128)(2,1)S(1)} %copy-done.3, s32[1,8]{1,0:T(1,128)S(1)} %copy-done.7, s32[1,8]{1,0:T(1,128)S(1)} %copy-done.8, ...), custom_call_target="tpu_custom_call" | custom-call | tf_op jit(solution)/shard_map/contrastive_adapter/pallas_call | solution.py:387
  77.3 0.6 copy.17
  77.9 0.6 copy.18
  78.5 0.6 copy.19
  79.1 0.6 copy.20
Async XLA Ops:
  0.6 2.0 %copy-start = (bf16[1,128,14336]{2,1,0:T(8,128)(2,1)S(1)}, bf16[1,128,14336]{2,1,0:T(8,128)(2,1)}, u32[]{:S(2)}) copy-start(bf16[1,128,14336]{2,1,0:T(8,128)(2,1)} %hid_hbm.1) | copy-start | bytes 11010052
  2.7 1.2 %copy-start.1 = (bf16[1,128,4096]{2,1,0:T(8,128)(2,1)S(1)}, bf16[1,128,4096]{2,1,0:T(8,128)(2,1)}, u32[]{:S(2)}) copy-start(bf16[1,128,4096]{2,1,0:T(8,128)(2,1)} %res_hbm.1) | copy-start | bytes 3145732
  3.9 0.8 %copy-start.2 = (bf16[1,8,4096]{2,1,0:T(8,128)(2,1)S(1)}, bf16[1,8,4096]{2,1,0:T(8,128)(2,1)}, u32[]{:S(2)}) copy-start(bf16[1,8,4096]{2,1,0:T(8,128)(2,1)} %q_in.1) | copy-start | bytes 196612
  4.7 0.8 %copy-start.3 = (bf16[1,8,4096]{2,1,0:T(8,128)(2,1)S(1)}, bf16[1,8,4096]{2,1,0:T(8,128)(2,1)}, u32[]{:S(2)}) copy-start(bf16[1,8,4096]{2,1,0:T(8,128)(2,1)} %p_in.1) | copy-start | bytes 196612
  5.6 0.7 copy-start.4
  6.3 0.7 copy-start.5
  7.0 0.7 copy-start.6
  7.7 0.7 copy-start.7
  8.4 0.7 copy-start.8

commit v2 on v1

--- a/solution.py
+++ b/solution.py
@@ -12,6 +12,7 @@
 SCALE = 50.0
 EXTRA = 1.3862943611198906
 EPS = 1e-06
+VMEM_BYTES = 64 * 1024 * 1024
 F32 = jnp.float32
 BF16 = jnp.bfloat16
 MESH = pl.DeviceIdType.MESH
@@ -58,19 +59,25 @@
     return jnp.concatenate([block[:, :half], block[:, half:]], axis=0)
 
 
+def farthest_first(ny, nz):
+    offsets = [(dy, dz) for dy in range(ny) for dz in range(nz) if dy or dz]
+    return sorted(offsets, key=lambda o: -(2 * min(o[0], ny - o[0]) + min(o[1], nz - o[1])))
+
+
 def kernel(
     ndp, nf,
-    q_in, p_in, pos_in, hard_in, gain_in, down_in, up_in, res_hbm, hid_hbm,
-    qg_out, pg_out, gd_out, gu_out,
-    hid, res, normed, unit_q, unit_p, gain_row,
+    q_hbm, p_hbm, pos_hbm, hard_hbm, gain_hbm, down_hbm, up_hbm, res_hbm, hid_hbm,
+    qg_hbm, pg_hbm, gd_hbm, gu_hbm,
+    qg_out, pg_out, gd_out, gu_out, q_in, p_in, pos_in, hard_in, gain_in, hid, res, normed, unit_q, unit_p, gain_row,
     eq, ep, rq, rp, pmat, qmat, ps, rs, rc, qs, rqr, pgs, rpg,
     rw, upf, sm, rmate, sa, ra, tiles, rb, rt,
-    sem, msem, asem,
+    sem, msem, in_sem, out_sem,
 ):
     nz = NZ
+    ny = ndp // nz
     ni = nf // 2
-    rank, dw = down_in.shape
-    uw = up_in.shape[1]
+    rank, dw = down_hbm.shape
+    uw = up_hbm.shape[1]
     sw = dw + uw
     d_model = unit_q.shape[1]
     fb = d_model // nz
@@ -98,10 +105,20 @@
             device_id=device, device_id_type=MESH,
         ).start()
 
-    load_hid = pltpu.make_async_copy(hid_hbm.at[0], hid, sem.at[0])
-    load_res = pltpu.make_async_copy(res_hbm.at[0], res, sem.at[1])
-    load_hid.start()
-    load_res.start()
+    started = []
+    own_w = rw.at[core, i0]
+    loads = [
+        pltpu.make_async_copy(src, dst, in_sem.at[k])
+        for k, (src, dst) in enumerate((
+            (p_hbm, p_in), (q_hbm, q_in),
+            (down_hbm, own_w.at[:, pl.ds(0, dw)]), (up_hbm, own_w.at[:, pl.ds(dw, uw)]),
+            (gain_hbm, gain_in), (pos_hbm, pos_in), (hard_hbm, hard_in),
+            (hid_hbm.at[0], hid), (res_hbm.at[0], res),
+        ))
+    ]
+    load_p, load_q, load_down, load_up, load_gain, load_pos, load_hard, load_hid, load_res = loads
+    for load in loads:
+        load.start()
 
     barrier = pltpu.get_barrier_semaphore()
 
@@ -121,17 +138,21 @@
             blocks[k] = stacked(unit[:, k * fb : (k + 1) * fb]).astype(BF16)
         return length
 
+    load_p.wait()
     len_p = unit_rows(p_in, unit_p, ep)
+    load_q.wait()
     len_q = unit_rows(q_in, unit_q, eq)
     rp[d] = ep[z]
     rq[z] = eq[z]
-    rw[core, i0] = jnp.concatenate([down_in[...], up_in[...]], axis=1)
+    load_down.wait()
+    load_up.wait()
 
     pl.semaphore_wait(barrier, (ndp - 1) + (ni - 1) + 1)
 
-    def send_p(k):
-        t = lax.rem(d + k, ndp)
-        send(ep.at[lax.rem(t, nz)], rp.at[d], sem.at[2], sem.at[3], (t, f))
+    def send_p(dy, dz):
+        tz = lax.rem(z + dz, nz)
+        t = lax.rem(y + dy, ny) * nz + tz
+        send(ep.at[tz], rp.at[d], sem.at[2], sem.at[3], (t, f))
 
     def send_q(k):
         tz = lax.rem(z + k, nz)
@@ -141,12 +162,40 @@
         i = lax.rem(i0 + k, ni)
         send(rw.at[core, i0], rw.at[core, i0], sem.at[6], sem.at[7], at_i(i))
 
-    loop(1, ndp, send_p)
+    for dy, dz in farthest_first(ny, nz):
+        send_p(dy, dz)
     loop(1, nz, send_q)
     loop(1, ni, send_w)
-
+    started += [
+        (rp.at[pl.ds(0, ndp - 1)], sem.at[2]), (rq.at[pl.ds(0, nz - 1)], sem.at[4]),
+        (rw.at[0, pl.ds(0, ni - 1)], sem.at[6]),
+    ]
+
+    load_gain.wait()
+    load_pos.wait()
+    load_hard.wait()
     for k in range(gain_in.shape[0]):
         gain_row[0:1, 128 * k : 128 * (k + 1)] = gain_in[...].astype(F32)[k : k + 1, :]
+
+    landed(rw.at[core, pl.ds(0, ni - 1)], sem.at[7])
+    send(rw.at[core], rw.at[core], sem.at[10], sem.at[11], mate)
+    started.append((rw.at[0], sem.at[10]))
+    load_hid.wait()
+
+    def reduce_part(c, start):
+        def step(i, acc):
+            cols = pl.ds(pl.multiple_of((2 * i + c) * dw, 128), dw)
+            return acc + dot(rw[c, i][:, :dw], hid[:, cols], 1, 1)
+
+        return lax.fori_loop(0, ni, step, start)
+
+    reduced_t = reduce_part(core, jnp.zeros((rank, seq), F32))
+    landed(rw.at[1 - core], sem.at[11])
+    reduced_t = reduce_part(1 - core, reduced_t).astype(BF16)
+    for c in range(2):
+        for i in range(ni):
+            at = (2 * i + c) * uw
+            upf[:, at : at + uw] = rw[c, i][:, dw:]
 
     landed(rq.at[pl.ds(0, nz - 1)], sem.at[5])
     landed(rp.at[pl.ds(0, ndp - 1)], sem.at[3])
@@ -163,19 +212,21 @@
         send(ps.at[tz], rs.at[z], sem.at[8], sem.at[9], at_z(tz))
 
     loop(1, nz, send_s)
-
-    landed(rw.at[core, pl.ds(0, ni - 1)], sem.at[7])
-    send(rw.at[core], rw.at[core], sem.at[10], sem.at[11], mate)
-    load_hid.wait()
-
-    def reduce_part(c, start):
-        def step(i, acc):
-            cols = pl.ds(pl.multiple_of((2 * i + c) * dw, 128), dw)
-            return acc + dot(rw[c, i][:, :dw], hid[:, cols], 1, 1)
-
-        return lax.fori_loop(0, ni, step, start)
-
-    reduced_t = reduce_part(core, jnp.zeros((rank, seq), F32))
+    started.append((rs.at[pl.ds(0, nz - 1)], sem.at[8]))
+
+    load_res.wait()
+    cw = 512 if d_model % 512 == 0 else 128
+    reduced = reduced_t.astype(F32).T.astype(BF16)
+
+    def forward(j, squares):
+        cols = pl.ds(pl.multiple_of(j * cw, 128), cw)
+        part = res[:, cols].astype(F32) + 2.0 * dot(reduced, upf[:, cols])
+        normed[:, cols] = part
+        return squares + jnp.sum(part * part, axis=1, keepdims=True)
+
+    squares = lax.fori_loop(0, d_model // cw, forward, jnp.zeros((seq, 1), F32))
+    inv_root = 1.0 / jnp.sqrt(squares / d_model + EPS)
+    inv_row = as_row(inv_root)
 
     landed(rs.at[pl.ds(0, nz - 1)], sem.at[9])
     ids = lax.broadcasted_iota(jnp.int32, (8, pg), 1)
@@ -192,48 +243,7 @@
         send(rc.at[z], rc.at[z], sem.at[12], sem.at[13], at_z(lax.rem(z + k, nz)))
 
     loop(1, nz, send_c)
-
-    landed(rw.at[1 - core], sem.at[11])
-    reduced_t = reduce_part(1 - core, reduced_t).astype(BF16)
-    for c in range(2):
-        for i in range(ni):
-            at = (2 * i + c) * uw
-            upf[:, at : at + uw] = rw[c, i][:, dw:]
-
-    landed(rc.at[pl.ds(0, nz - 1)], sem.at[13])
-    cmat = jnp.concatenate(split_rows(rc), axis=1)
-    for h in range(2):
-        qs[:, :, h * hw : (h + 1) * hw] = (SCALE * dot(cmat, pmat[h])).reshape(nz, 8, hw)
-    rqr[z] = qs[z]
-
-    def send_qr(k):
-        tz = lax.rem(z + k, nz)
-        send(qs.at[tz], rqr.at[z], sem.at[14], sem.at[15], at_z(tz))
-
-    loop(1, nz, send_qr)
-    terms = [(SCALE * dot(cmat, qmat[h], 0, 0)).reshape(ndp, 8, hw) for h in range(2)]
-    pgs[...] = jnp.concatenate(terms, axis=1).astype(BF16)
-    rpg[d] = pgs[d]
-
-    def send_pg(k):
-        t = lax.rem(d + k, ndp)
-        send(pgs.at[t], rpg.at[d], sem.at[16], sem.at[17], (t, f))
-
-    loop(1, ndp, send_pg)
-
-    load_res.wait()
-    cw = 512 if d_model % 512 == 0 else 128
-    reduced = reduced_t.astype(F32).T.astype(BF16)
-
-    def forward(j, squares):
-        cols = pl.ds(pl.multiple_of(j * cw, 128), cw)
-        part = res[:, cols].astype(F32) + 2.0 * dot(reduced, upf[:, cols])
-        normed[:, cols] = part
-        return squares + jnp.sum(part * part, axis=1, keepdims=True)
-
-    squares = lax.fori_loop(0, d_model // cw, forward, jnp.zeros((seq, 1), F32))
-    inv_root = 1.0 / jnp.sqrt(squares / d_model + EPS)
-    inv_row = as_row(inv_root)
+    started.append((rc.at[pl.ds(0, nz - 1)], sem.at[12]))
 
     def normalize(j, acc):
         cols = pl.ds(pl.multiple_of(j * cw, 128), cw)
@@ -245,6 +255,23 @@
 
     normed_up = lax.fori_loop(0, d_model // cw, normalize, jnp.zeros((rank, seq), F32))
 
+    landed(rc.at[pl.ds(0, nz - 1)], sem.at[13])
+    cmat = jnp.concatenate(split_rows(rc), axis=1)
+    for h in range(2):
+        qs[:, :, h * hw : (h + 1) * hw] = (SCALE * dot(cmat, pmat[h])).reshape(nz, 8, hw)
+    rqr[z] = qs[z]
+
+    def send_qr(k):
+        tz = lax.rem(z + k, nz)
+        send(qs.at[tz], rqr.at[z], sem.at[14], sem.at[15], at_z(tz))
+
+    loop(1, nz, send_qr)
+    started.append((rqr.at[pl.ds(0, nz - 1)], sem.at[14]))
+    terms = [(SCALE * dot(cmat, qmat[h], 0, 0)).reshape(ndp, 8, hw) for h in range(2)]
+    pgs[...] = jnp.concatenate(terms, axis=1).astype(BF16)
+    rpg[d] = pgs[d]
+
+
     landed(rqr.at[pl.ds(0, nz - 1)], sem.at[15])
 
     def tangent(unit_ref, pieces, length, out_ref):
@@ -254,7 +281,12 @@
         out_ref[0] = full.astype(BF16)
         return full
 
+    stores = [
+        pltpu.make_async_copy(src, dst, out_sem.at[k])
+        for k, (src, dst) in enumerate(((qg_out, qg_hbm), (pg_out, pg_hbm), (gd_out, gd_hbm), (gu_out, gu_hbm)))
+    ]
     query_full = tangent(unit_q, [rqr[k] for k in range(nz)], len_q, qg_out)
+    stores[0].start()
 
     grad_norm = gain_row[...] * query_full[0:1, :] * (1.0 / seq)
     projected = jnp.sum(normed[...] * grad_norm, axis=1, keepdims=True) * (1.0 / d_model)
@@ -282,6 +314,7 @@
         for_mate(lax.rem(i0 + k, ni))
 
     loop(1, ni + 1, mate_step)
+    started.append((sm, sem.at[18]))
 
     def own_terms(i, out_ref, out_at):
         down_term, up_term = terms_of(i, core)
@@ -296,7 +329,15 @@
         send(sa.at[i], ra.at[i0], sem.at[19], sem.at[20], at_i(i))
 
     loop(1, ni, own_step)
+    started.append((sa.at[pl.ds(0, ni - 1)], sem.at[19]))
     own_terms(i0, ra, i0)
+
+    def send_pg(k):
+        t = lax.rem(d + k, ndp)
+        send(pgs.at[t], rpg.at[d], sem.at[16], sem.at[17], (t, f))
+
+    loop(1, ndp, send_pg)
+    started.append((rpg.at[pl.ds(0, ndp - 1)], sem.at[16]))
 
     landed(ra.at[pl.ds(0, ni - 1)], sem.at[20])
     total = jnp.sum(ra[...].astype(F32), axis=0)
@@ -324,6 +365,7 @@
             both = both + rpg[a * nz + k].astype(F32)
         pieces += [both[:8], both[8:]]
     tangent(unit_p, pieces, len_p, pg_out)
+    stores[1].start()
 
     @pl.when(is_owner)
     def _():
@@ -349,17 +391,11 @@
         else:
             at = 128 * c - dw
             gu_out[8 * h : 8 * h + 8, at : at + 128] = rt[k]
-
-    landed(rp.at[pl.ds(0, ndp - 1)], sem.at[2])
-    landed(rq.at[pl.ds(0, nz - 1)], sem.at[4])
-    landed(rw.at[0, pl.ds(0, ni - 1)], sem.at[6])
-    landed(rs.at[pl.ds(0, nz - 1)], sem.at[8])
-    landed(rw.at[0], sem.at[10])
-    landed(rc.at[pl.ds(0, nz - 1)], sem.at[12])
-    landed(rqr.at[pl.ds(0, nz - 1)], sem.at[14])
-    landed(rpg.at[pl.ds(0, ndp - 1)], sem.at[16])
-    landed(sm, sem.at[18])
-    landed(sa.at[pl.ds(0, ni - 1)], sem.at[19])
+    stores[2].start()
+    stores[3].start()
+
+    for ref, left in started:
+        landed(ref, left)
 
     @pl.when(is_owner)
     def _():
@@ -369,6 +405,22 @@
     @pl.when(jnp.logical_not(is_owner))
     def _():
         landed(tiles, sem.at[21])
+
+    for store in stores:
+        store.wait()
+
+
+def store_kernel(*refs):
+    sources, results, staged, sem = refs[:4], refs[4:8], refs[8:12], refs[12]
+    loads = [pltpu.make_async_copy(sources[k], staged[k], sem.at[0, k]) for k in range(4)]
+    stores = [pltpu.make_async_copy(staged[k], results[k], sem.at[1, k]) for k in range(4)]
+    for load in loads:
+        load.start()
+    for load, store in zip(loads, stores):
+        load.wait()
+        store.start()
+    for store in stores:
+        store.wait()
 
 
 def per_device(ndp, nf, queries, passages, positives, hard_blocks, residual, hidden_act, gain, down_rows, up_rows):
@@ -382,9 +434,8 @@
     hw = fb // 2
     pg = ndp * 8
     n_tiles = (rank // 8) * (sw // 128)
-    vmem = pl.BlockSpec(memory_space=pltpu.VMEM)
-    anywhere = pl.BlockSpec(memory_space=pl.ANY)
-    return pl.pallas_call(
+    hbm = pl.BlockSpec(memory_space=pltpu.HBM)
+    results = pl.pallas_call(
         functools.partial(kernel, ndp, nf),
         out_shape=(
             jax.ShapeDtypeStruct(queries.shape, BF16),
@@ -392,9 +443,18 @@
             jax.ShapeDtypeStruct(down_rows.shape, F32),
             jax.ShapeDtypeStruct(up_rows.shape, F32),
         ),
-        in_specs=[vmem] * 7 + [anywhere] * 2,
-        out_specs=(vmem,) * 4,
+        in_specs=[hbm] * 9,
+        out_specs=(hbm,) * 4,
         scratch_shapes=[
+            pltpu.VMEM(queries.shape, BF16),
+            pltpu.VMEM(passages.shape, BF16),
+            pltpu.VMEM(down_rows.shape, F32),
+            pltpu.VMEM(up_rows.shape, F32),
+            pltpu.VMEM(queries.shape, BF16),
+            pltpu.VMEM(passages.shape, BF16),
+            pltpu.VMEM(positives.shape, jnp.int32),
+            pltpu.VMEM(hard_blocks.shape, jnp.int32),
+            pltpu.VMEM((d_model // 128, 128), BF16),
             pltpu.VMEM((seq, hid), BF16),
             pltpu.VMEM((seq, d_model), BF16),
             pltpu.VMEM((seq, d_model), F32),
@@ -425,16 +485,26 @@
             pltpu.VMEM((n_tiles, 8, 128), F32),
             pltpu.SemaphoreType.DMA((25,)),
             pltpu.SemaphoreType.DMA((ni,)),
-            pltpu.SemaphoreType.DMA((1,)),
+            pltpu.SemaphoreType.DMA((9,)),
+            pltpu.SemaphoreType.DMA((4,)),
         ],
         compiler_params=pltpu.CompilerParams(
-            collective_id=0, has_side_effects=True, vmem_limit_bytes=40 * 1024 * 1024
+            collective_id=0, has_side_effects=True, vmem_limit_bytes=VMEM_BYTES
         ),
         name="contrastive_adapter",
     )(
         queries, passages, positives, hard_blocks, gain.reshape(d_model // 128, 128),
         down_rows, up_rows, residual, hidden_act,
     )
+    return pl.pallas_call(
+        store_kernel,
+        out_shape=tuple(jax.ShapeDtypeStruct(r.shape, r.dtype) for r in results),
+        in_specs=[hbm] * 4,
+        out_specs=(hbm,) * 4,
+        scratch_shapes=[pltpu.VMEM(r.shape, r.dtype) for r in results] + [pltpu.SemaphoreType.DMA((2, 4))],
+        compiler_params=pltpu.CompilerParams(vmem_limit_bytes=VMEM_BYTES),
+        name="store_results",
+    )(*results)
 
 
 def solution(mesh):

time: 80.2 us -> 74.2 us (0.925)
  the two profiles are of different devices: /device:TPU:4 before, /device:TPU:8 now
where the time goes in v2:
time: 74.2 us; the launch traced here: 74 us
  Pallas kernels  73.4 us (99%)
    pallas_call x1, Pallas kernels, per_device(): pl.pallas_call(functools.partial(kernel, ndp, nf), out_shape=(jax.ShapeDt...  71.8 us
    pallas_call x1, Pallas kernels, per_device(): pl.pallas_call(store_kernel, out_shape=tuple((jax.ShapeDtypeStruct(r.shap...  1.59 us

profile of v2, /device:TPU:8, one launch (start us, length us, event | category | flops | bytes accessed | tf_op | source)
XLA Modules:
  0.0 74.0 jit_solution(2075314362534246264)
XLA Ops:
  0.6 71.8 %contrastive_adapter.1 = (bf16[1,8,4096]{2,1,0:T(8,128)(2,1)}, bf16[1,8,4096]{2,1,0:T(8,128)(2,1)}, f32[16,896]{1,0:T(8,128)}, f32[16,256]{1,0:T(8,128)}) custom-call(bf16[1,8,4096]{2,1,0:T(8,128)(2,1)} %q_hbm.1, bf16[1,8,4096]{2,1,0:T(8,128)(2,1)} %p_hbm.1, s32[1,8]{1,0:T(1,128)} %pos_hbm.1, s32[1,8]{1,0:T(1,128)} %hard_hbm.1, bf16[32,128]{1,0:T(8,128)(2,1)} %bitcast.1, ...), custom_call_target="tpu_custom_call" | custom-call | tf_op jit(solution)/shard_map/contrastive_adapter/pallas_call | solution.py:438
  72.5 1.6 %store_results.1 = (bf16[1,8,4096]{2,1,0:T(8,128)(2,1)}, bf16[1,8,4096]{2,1,0:T(8,128)(2,1)}, f32[16,896]{1,0:T(8,128)}, f32[16,256]{1,0:T(8,128)}) custom-call(bf16[1,8,4096]{2,1,0:T(8,128)(2,1)} %get-tuple-element.8.refs_0_, bf16[1,8,4096]{2,1,0:T(8,128)(2,1)} %get-tuple-element.9.refs_1_, f32[16,896]{1,0:T(8,128)} %get-tuple-element.10.refs_2_, ...), custom_call_target="tpu_custom_call" | custom-call | tf_op jit(solution)/shard_map/store_results/pallas_call | solution.py:499

commit v3 on v2

--- a/solution.py
+++ b/solution.py
@@ -12,7 +12,7 @@
 SCALE = 50.0
 EXTRA = 1.3862943611198906
 EPS = 1e-06
-VMEM_BYTES = 64 * 1024 * 1024
+VMEM_BYTES = 48 * 1024 * 1024
 F32 = jnp.float32
 BF16 = jnp.bfloat16
 MESH = pl.DeviceIdType.MESH
@@ -26,12 +26,12 @@
     pltpu.make_async_copy(ref, ref, sem).wait()
 
 
-def loop(low, high, body):
+def loop(low, high, body, unroll=1):
     def step(k, carry):
         body(k)
         return carry
 
-    lax.fori_loop(low, high, step, 0)
+    lax.fori_loop(low, high, step, 0, unroll=unroll)
 
 
 def as_column(row):
@@ -67,11 +67,11 @@
 def kernel(
     ndp, nf,
     q_hbm, p_hbm, pos_hbm, hard_hbm, gain_hbm, down_hbm, up_hbm, res_hbm, hid_hbm,
-    qg_hbm, pg_hbm, gd_hbm, gu_hbm,
-    qg_out, pg_out, gd_out, gu_out, q_in, p_in, pos_in, hard_in, gain_in, hid, res, normed, unit_q, unit_p, gain_row,
-    eq, ep, rq, rp, pmat, qmat, ps, rs, rc, qs, rqr, pgs, rpg,
+    qg_out, pg_out, gd_out, gu_out,
+    q_in, p_in, pos_in, hard_in, gain_in, hid, res, normed, unit_q, unit_p, gain_row,
+    eq, ep, rq, rp, pmat, qmat, ps, rs, rtag, rsc, qc, rqc, rc, qs, rqr, pgs, rpg,
     rw, upf, sm, rmate, sa, ra, tiles, rb, rt,
-    sem, msem, in_sem, out_sem,
+    sem, msem, in_sem,
 ):
     nz = NZ
     ny = ndp // nz
@@ -117,17 +117,20 @@
         ))
     ]
     load_p, load_q, load_down, load_up, load_gain, load_pos, load_hard, load_hid, load_res = loads
-    for load in loads:
-        load.start()
+    load_p.start()
+    load_q.start()
 
     barrier = pltpu.get_barrier_semaphore()
 
     def greet(device):
         pl.semaphore_signal(barrier, inc=1, device_id=device, device_id_type=MESH)
 
-    loop(1, ndp, lambda k: greet((lax.rem(d + k, ndp), f)))
+    for dy, dz in farthest_first(ny, nz):
+        greet((lax.rem(y + dy, ny) * nz + lax.rem(z + dz, nz), f))
     loop(1, ni, lambda k: greet(at_i(lax.rem(i0 + k, ni))))
     greet(mate)
+    for load in loads[2:]:
+        load.start()
 
     def unit_rows(ref, unit_ref, blocks):
         rows = ref[0].astype(F32)
@@ -146,6 +149,12 @@
     rq[z] = eq[z]
     load_down.wait()
     load_up.wait()
+    load_pos.wait()
+    load_hard.wait()
+    pos = as_column(pos_in[...].astype(F32))
+    hard = as_column(hard_in[...].astype(F32))
+    tag = jnp.where(lax.broadcasted_iota(jnp.int32, (8, 128), 1) < 64, pos[0:1], hard[0:1])
+    rtag[z] = jnp.where(lax.broadcasted_iota(jnp.int32, (8, 128), 0) == z, tag, 0.0)
 
     pl.semaphore_wait(barrier, (ndp - 1) + (ni - 1) + 1)
 
@@ -157,6 +166,7 @@
     def send_q(k):
         tz = lax.rem(z + k, nz)
         send(eq.at[tz], rq.at[z], sem.at[4], sem.at[5], at_z(tz))
+        send(rtag.at[z], rtag.at[z], sem.at[25], sem.at[26], at_z(tz))
 
     def send_w(k):
         i = lax.rem(i0 + k, ni)
@@ -167,13 +177,12 @@
     loop(1, nz, send_q)
     loop(1, ni, send_w)
     started += [
+        (rtag.at[pl.ds(0, nz - 1)], sem.at[25]),
         (rp.at[pl.ds(0, ndp - 1)], sem.at[2]), (rq.at[pl.ds(0, nz - 1)], sem.at[4]),
         (rw.at[0, pl.ds(0, ni - 1)], sem.at[6]),
     ]
 
     load_gain.wait()
-    load_pos.wait()
-    load_hard.wait()
     for k in range(gain_in.shape[0]):
         gain_row[0:1, 128 * k : 128 * (k + 1)] = gain_in[...].astype(F32)[k : k + 1, :]
 
@@ -198,6 +207,7 @@
             upf[:, at : at + uw] = rw[c, i][:, dw:]
 
     landed(rq.at[pl.ds(0, nz - 1)], sem.at[5])
+    landed(rtag.at[pl.ds(0, nz - 1)], sem.at[26])
     landed(rp.at[pl.ds(0, ndp - 1)], sem.at[3])
     for h, half in enumerate(split_rows(rp)):
         pmat[h] = half
@@ -206,16 +216,17 @@
     partial = dot(qmat[0], pmat[0], 1, 1) + dot(qmat[1], pmat[1], 1, 1)
     ps[...] = partial.reshape(nz, 8, pg)
     rs[z] = ps[z]
-
-    def send_s(k):
-        tz = lax.rem(z + k, nz)
-        send(ps.at[tz], rs.at[z], sem.at[8], sem.at[9], at_z(tz))
-
-    loop(1, nz, send_s)
-    started.append((rs.at[pl.ds(0, nz - 1)], sem.at[8]))
+    for k in range(nz):
+        rsc[z, k : k + 1, :] = ps[k, 0:1, :]
+
+    def send_sc(k):
+        send(rsc.at[z], rsc.at[z], sem.at[27], sem.at[28], at_z(lax.rem(z + k, nz)))
+
+    loop(1, nz, send_sc)
+    started.append((rsc.at[pl.ds(0, nz - 1)], sem.at[27]))
 
     load_res.wait()
-    cw = 512 if d_model % 512 == 0 else 128
+    cw = d_model // 4
     reduced = reduced_t.astype(F32).T.astype(BF16)
 
     def forward(j, squares):
@@ -228,22 +239,35 @@
     inv_root = 1.0 / jnp.sqrt(squares / d_model + EPS)
     inv_row = as_row(inv_root)
 
-    landed(rs.at[pl.ds(0, nz - 1)], sem.at[9])
-    ids = lax.broadcasted_iota(jnp.int32, (8, pg), 1)
-    pos = as_column(pos_in[...].astype(F32))
-    hard = as_column(hard_in[...].astype(F32))
-    blocks = lax.shift_right_logical(ids, 2).astype(F32)
-    logits = SCALE * jnp.sum(rs[...], axis=0) + jnp.where(blocks == hard, EXTRA, 0.0)
-    weights = jnp.exp(logits)
-    soft = weights / jnp.sum(weights, axis=1, keepdims=True)
-    coeffs = soft - jnp.where(ids.astype(F32) == pos, 1.0, 0.0)
-    rc[z] = stacked(coeffs).astype(BF16)
-
-    def send_c(k):
-        send(rc.at[z], rc.at[z], sem.at[12], sem.at[13], at_z(lax.rem(z + k, nz)))
-
-    loop(1, nz, send_c)
-    started.append((rc.at[pl.ds(0, nz - 1)], sem.at[12]))
+    def coefficients(products, positive, hard_block):
+        ids = lax.broadcasted_iota(jnp.int32, products.shape, 1)
+        blocks = lax.shift_right_logical(ids, 2).astype(F32)
+        weights = jnp.exp(SCALE * products + jnp.where(blocks == hard_block, EXTRA, 0.0))
+        soft = weights / jnp.sum(weights, axis=1, keepdims=True)
+        return soft - jnp.where(ids.astype(F32) == positive, 1.0, 0.0)
+
+    landed(rsc.at[pl.ds(0, nz - 1)], sem.at[28])
+    tags = jnp.sum(rtag[...], axis=0)[:nz]
+    first = coefficients(jnp.sum(rsc[...], axis=0), tags[:, 0:1], tags[:, 64:65]).astype(BF16)
+    for h in range(2):
+        term = SCALE * dot(first, pmat[h])
+        for k in range(hw // 128):
+            qc[:, h * (hw // 128) + k, :] = term[:, 128 * k : 128 * k + 128]
+    rqc[z] = qc[z]
+
+    def send_qc(k):
+        tz = lax.rem(z + k, nz)
+        send(qc.at[tz], rqc.at[z], sem.at[29], sem.at[30], at_z(tz))
+
+    loop(1, nz, send_qc)
+    started.append((rqc.at[pl.ds(0, nz - 1)], sem.at[29]))
+
+    def send_s(k):
+        tz = lax.rem(z + k, nz)
+        send(ps.at[tz], rs.at[z], sem.at[8], sem.at[9], at_z(tz))
+
+    loop(1, nz, send_s)
+    started.append((rs.at[pl.ds(0, nz - 1)], sem.at[8]))
 
     def normalize(j, acc):
         cols = pl.ds(pl.multiple_of(j * cw, 128), cw)
@@ -255,40 +279,14 @@
 
     normed_up = lax.fori_loop(0, d_model // cw, normalize, jnp.zeros((rank, seq), F32))
 
-    landed(rc.at[pl.ds(0, nz - 1)], sem.at[13])
-    cmat = jnp.concatenate(split_rows(rc), axis=1)
-    for h in range(2):
-        qs[:, :, h * hw : (h + 1) * hw] = (SCALE * dot(cmat, pmat[h])).reshape(nz, 8, hw)
-    rqr[z] = qs[z]
-
-    def send_qr(k):
-        tz = lax.rem(z + k, nz)
-        send(qs.at[tz], rqr.at[z], sem.at[14], sem.at[15], at_z(tz))
-
-    loop(1, nz, send_qr)
-    started.append((rqr.at[pl.ds(0, nz - 1)], sem.at[14]))
-    terms = [(SCALE * dot(cmat, qmat[h], 0, 0)).reshape(ndp, 8, hw) for h in range(2)]
-    pgs[...] = jnp.concatenate(terms, axis=1).astype(BF16)
-    rpg[d] = pgs[d]
-
-
-    landed(rqr.at[pl.ds(0, nz - 1)], sem.at[15])
-
-    def tangent(unit_ref, pieces, length, out_ref):
-        raw = jnp.concatenate(pieces, axis=1)
-        unit = unit_ref[...]
-        full = (raw - unit * jnp.sum(unit * raw, axis=1, keepdims=True)) / length
-        out_ref[0] = full.astype(BF16)
-        return full
-
-    stores = [
-        pltpu.make_async_copy(src, dst, out_sem.at[k])
-        for k, (src, dst) in enumerate(((qg_out, qg_hbm), (pg_out, pg_hbm), (gd_out, gd_hbm), (gu_out, gu_hbm)))
-    ]
-    query_full = tangent(unit_q, [rqr[k] for k in range(nz)], len_q, qg_out)
-    stores[0].start()
-
-    grad_norm = gain_row[...] * query_full[0:1, :] * (1.0 / seq)
+    def tangent(unit, raw, length):
+        return (raw - unit * jnp.sum(unit * raw, axis=1, keepdims=True)) / length
+
+    landed(rqc.at[pl.ds(0, nz - 1)], sem.at[30])
+    first_raw = jnp.concatenate([rqc[k, c : c + 1, :] for k in range(nz) for c in range(fb // 128)], axis=1)
+    upstream = tangent(unit_q[0:1, :], first_raw, len_q[0:1, :])
+
+    grad_norm = gain_row[...] * upstream * (1.0 / seq)
     projected = jnp.sum(normed[...] * grad_norm, axis=1, keepdims=True) * (1.0 / d_model)
     up_grad = jnp.sum(upf[...].astype(F32) * grad_norm, axis=1, keepdims=True)
     grad_reduced_t = (2.0 * (up_grad - as_row(projected) * normed_up) * inv_row).astype(BF16)
@@ -313,7 +311,7 @@
     def mate_step(k):
         for_mate(lax.rem(i0 + k, ni))
 
-    loop(1, ni + 1, mate_step)
+    loop(1, ni + 1, mate_step, unroll=ni)
     started.append((sm, sem.at[18]))
 
     def own_terms(i, out_ref, out_at):
@@ -328,16 +326,19 @@
         own_terms(i, sa, i)
         send(sa.at[i], ra.at[i0], sem.at[19], sem.at[20], at_i(i))
 
-    loop(1, ni, own_step)
+    loop(1, ni, own_step, unroll=ni - 1)
     started.append((sa.at[pl.ds(0, ni - 1)], sem.at[19]))
     own_terms(i0, ra, i0)
 
-    def send_pg(k):
-        t = lax.rem(d + k, ndp)
-        send(pgs.at[t], rpg.at[d], sem.at[16], sem.at[17], (t, f))
-
-    loop(1, ndp, send_pg)
-    started.append((rpg.at[pl.ds(0, ndp - 1)], sem.at[16]))
+    landed(rs.at[pl.ds(0, nz - 1)], sem.at[9])
+    coeffs = coefficients(jnp.sum(rs[...], axis=0), pos, hard)
+    rc[z] = stacked(coeffs).astype(BF16)
+
+    def send_c(k):
+        send(rc.at[z], rc.at[z], sem.at[12], sem.at[13], at_z(lax.rem(z + k, nz)))
+
+    loop(1, nz, send_c)
+    started.append((rc.at[pl.ds(0, nz - 1)], sem.at[12]))
 
     landed(ra.at[pl.ds(0, ni - 1)], sem.at[20])
     total = jnp.sum(ra[...].astype(F32), axis=0)
@@ -357,15 +358,28 @@
 
     loop(0, n_tiles, send_tile)
 
-    landed(rpg.at[pl.ds(0, ndp - 1)], sem.at[17])
-    pieces = []
-    for k in range(nz):
-        both = rpg[k].astype(F32)
-        for a in range(1, ndp // nz):
-            both = both + rpg[a * nz + k].astype(F32)
-        pieces += [both[:8], both[8:]]
-    tangent(unit_p, pieces, len_p, pg_out)
-    stores[1].start()
+    landed(rc.at[pl.ds(0, nz - 1)], sem.at[13])
+    cmat = jnp.concatenate(split_rows(rc), axis=1)
+    for h in range(2):
+        qs[:, :, h * hw : (h + 1) * hw] = (SCALE * dot(cmat, pmat[h])).reshape(nz, 8, hw)
+    rqr[z] = qs[z]
+
+    def send_qr(k):
+        tz = lax.rem(z + k, nz)
+        send(qs.at[tz], rqr.at[z], sem.at[14], sem.at[15], at_z(tz))
+
+    loop(1, nz, send_qr)
+    started.append((rqr.at[pl.ds(0, nz - 1)], sem.at[14]))
+    terms = [(SCALE * dot(cmat, qmat[h], 0, 0)).reshape(ndp, 8, hw) for h in range(2)]
+    pgs[...] = jnp.concatenate(terms, axis=1).astype(BF16)
+    rpg[d] = pgs[d]
+
+    def send_pg(k):
+        t = lax.rem(d + k, ndp)
+        send(pgs.at[t], rpg.at[d], sem.at[16], sem.at[17], (t, f))
+
+    loop(1, ndp, send_pg)
+    started.append((rpg.at[pl.ds(0, ndp - 1)], sem.at[16]))
 
     @pl.when(is_owner)
     def _():
@@ -373,11 +387,26 @@
         landed(rb.at[pl.ds(0, ndp - 1)], sem.at[22])
         rt[own_tile] = jnp.sum(rb[...], axis=0)
 
-        def send_total(k):
-            t = lax.rem(d + k, ndp)
+        for dy, dz in farthest_first(ny, nz):
+            t = lax.rem(y + dy, ny) * nz + lax.rem(z + dz, nz)
             send(rt.at[own_tile], rt.at[own_tile], sem.at[23], sem.at[24], (t, f))
 
-        loop(1, ndp, send_total)
+
+    landed(rqr.at[pl.ds(0, nz - 1)], sem.at[15])
+    raw = jnp.concatenate([rqr[k] for k in range(nz)], axis=1)
+    qg_out[0] = tangent(unit_q[...], raw, len_q).astype(BF16)
+
+    landed(rpg.at[pl.ds(0, ndp - 1)], sem.at[17])
+    pieces = []
+    for k in range(nz):
+        both = rpg[k].astype(F32)
+        for a in range(1, ny):
+            both = both + rpg[a * nz + k].astype(F32)
+        pieces += [both[:8], both[8:]]
+    pg_out[0] = tangent(unit_p[...], jnp.concatenate(pieces, axis=1), len_p).astype(BF16)
+
+    @pl.when(is_owner)
+    def _():
         landed(rt.at[pl.ds(0, n_tiles - 1)], sem.at[24])
 
     @pl.when(jnp.logical_not(is_owner))
@@ -391,8 +420,6 @@
         else:
             at = 128 * c - dw
             gu_out[8 * h : 8 * h + 8, at : at + 128] = rt[k]
-    stores[2].start()
-    stores[3].start()
 
     for ref, left in started:
         landed(ref, left)
@@ -406,18 +433,11 @@
     def _():
         landed(tiles, sem.at[21])
 
+
+def store_kernel(*refs):
+    sources, results, sem = refs[:4], refs[4:8], refs[8]
+    stores = [pltpu.make_async_copy(sources[k], results[k], sem.at[k]) for k in range(4)]
     for store in stores:
-        store.wait()
-
-
-def store_kernel(*refs):
-    sources, results, staged, sem = refs[:4], refs[4:8], refs[8:12], refs[12]
-    loads = [pltpu.make_async_copy(sources[k], staged[k], sem.at[0, k]) for k in range(4)]
-    stores = [pltpu.make_async_copy(staged[k], results[k], sem.at[1, k]) for k in range(4)]
-    for load in loads:
-        load.start()
-    for load, store in zip(loads, stores):
-        load.wait()
         store.start()
     for store in stores:
         store.wait()
@@ -435,21 +455,22 @@
     pg = ndp * 8
     n_tiles = (rank // 8) * (sw // 128)
     hbm = pl.BlockSpec(memory_space=pltpu.HBM)
+    vmem = pl.BlockSpec(memory_space=pltpu.VMEM)
+    operands = (
+        queries, passages, positives, hard_blocks, gain.reshape(d_model // 128, 128),
+        down_rows, up_rows, residual, hidden_act,
+    )
     results = pl.pallas_call(
         functools.partial(kernel, ndp, nf),
         out_shape=(
-            jax.ShapeDtypeStruct(queries.shape, BF16),
-            jax.ShapeDtypeStruct(passages.shape, BF16),
-            jax.ShapeDtypeStruct(down_rows.shape, F32),
-            jax.ShapeDtypeStruct(up_rows.shape, F32),
-        ),
-        in_specs=[hbm] * 9,
-        out_specs=(hbm,) * 4,
-        scratch_shapes=[
             pltpu.VMEM(queries.shape, BF16),
             pltpu.VMEM(passages.shape, BF16),
             pltpu.VMEM(down_rows.shape, F32),
             pltpu.VMEM(up_rows.shape, F32),
+        ),
+        in_specs=[hbm] * 9,
+        out_specs=(vmem,) * 4,
+        scratch_shapes=[
             pltpu.VMEM(queries.shape, BF16),
             pltpu.VMEM(passages.shape, BF16),
             pltpu.VMEM(positives.shape, jnp.int32),
@@ -469,6 +490,10 @@
             pltpu.VMEM((2, 8 * NZ, hw), BF16),
             pltpu.VMEM((NZ, 8, pg), F32),
             pltpu.VMEM((NZ, 8, pg), F32),
+            pltpu.VMEM((NZ, 8, 128), F32),
+            pltpu.VMEM((NZ, NZ, pg), F32),
+            pltpu.VMEM((NZ, fb // 128, 128), F32),
+            pltpu.VMEM((NZ, fb // 128, 128), F32),
             pltpu.VMEM((NZ, 16, pg // 2), BF16),
             pltpu.VMEM((NZ, 8, fb), F32),
             pltpu.VMEM((NZ, 8, fb), F32),
@@ -483,26 +508,21 @@
             pltpu.VMEM((n_tiles, 8, 128), F32),
             pltpu.VMEM((ndp, 8, 128), F32),
             pltpu.VMEM((n_tiles, 8, 128), F32),
-            pltpu.SemaphoreType.DMA((25,)),
+            pltpu.SemaphoreType.DMA((31,)),
             pltpu.SemaphoreType.DMA((ni,)),
             pltpu.SemaphoreType.DMA((9,)),
-            pltpu.SemaphoreType.DMA((4,)),
         ],
         compiler_params=pltpu.CompilerParams(
             collective_id=0, has_side_effects=True, vmem_limit_bytes=VMEM_BYTES
         ),
         name="contrastive_adapter",
-    )(
-        queries, passages, positives, hard_blocks, gain.reshape(d_model // 128, 128),
-        down_rows, up_rows, residual, hidden_act,
-    )
+    )(*(pltpu.with_memory_space_constraint(x, pltpu.HBM) for x in operands))
     return pl.pallas_call(
         store_kernel,
         out_shape=tuple(jax.ShapeDtypeStruct(r.shape, r.dtype) for r in results),
-        in_specs=[hbm] * 4,
+        in_specs=[vmem] * 4,
         out_specs=(hbm,) * 4,
-        scratch_shapes=[pltpu.VMEM(r.shape, r.dtype) for r in results] + [pltpu.SemaphoreType.DMA((2, 4))],
-        compiler_params=pltpu.CompilerParams(vmem_limit_bytes=VMEM_BYTES),
+        scratch_shapes=[pltpu.SemaphoreType.DMA((4,))],
         name="store_results",
     )(*results)
 

time: 74.2 us -> 71.8 us (0.968)
  the two profiles are of different devices: /device:TPU:8 before, /device:TPU:2 now
where the time goes in v3:
time: 71.8 us; the launch traced here: 71.6 us
  Pallas kernels  68.5 us (95%)
  local copies, waits for them, and re-layouts  2.45 us (3%)
    pallas_call x1, Pallas kernels, per_device(): pl.pallas_call(functools.partial(kernel, ndp, nf), out_shape=(pltpu.VMEM(...  66.9 us
    unnamed x8, local copies, waits for them, and re-layouts  2.45 us
    pallas_call x1, Pallas kernels, per_device(): pl.pallas_call(store_kernel, out_shape=tuple((jax.ShapeDtypeStruct(r.shap...  1.58 us

profile of v3, /device:TPU:2, one launch (start us, length us, event | category | flops | bytes accessed | tf_op | source)
XLA Modules:
  0.0 71.6 jit_solution(9468793181158871323)
XLA Ops:
  0.6 66.9 %contrastive_adapter.1 = (bf16[1,8,4096]{2,1,0:T(8,128)(2,1)S(1)}, bf16[1,8,4096]{2,1,0:T(8,128)(2,1)S(1)}, f32[16,896]{1,0:T(8,128)S(1)}, f32[16,256]{1,0:T(8,128)S(1)}) custom-call(bf16[1,8,4096]{2,1,0:T(8,128)(2,1)} %q_hbm.1, bf16[1,8,4096]{2,1,0:T(8,128)(2,1)} %p_hbm.1, s32[1,8]{1,0:T(1,128)} %pos_hbm.1, s32[1,8]{1,0:T(1,128)} %hard_hbm.1, ...), custom_call_target="tpu_custom_call" | custom-call | tf_op jit(solution)/shard_map/contrastive_adapter/pallas_call | solution.py:463
  67.5 0.0 copy-start
  67.5 0.6 copy-done
  68.1 0.0 copy-start.1
  68.2 0.6 copy-done.1
  68.8 0.0 copy-start.2
  68.8 0.6 copy-done.2
  69.4 0.0 copy-start.3
  69.4 0.6 copy-done.3
  70.0 1.6 %store_results.1 = (bf16[1,8,4096]{2,1,0:T(8,128)(2,1)}, bf16[1,8,4096]{2,1,0:T(8,128)(2,1)}, f32[16,896]{1,0:T(8,128)}, f32[16,256]{1,0:T(8,128)}) custom-call(bf16[1,8,4096]{2,1,0:T(8,128)(2,1)} %copy-done, bf16[1,8,4096]{2,1,0:T(8,128)(2,1)} %copy-done.1, f32[16,896]{1,0:T(8,128)} %copy-done.2, f32[16,256]{1,0:T(8,128)} %copy-done.3), custom_call_target="tpu_custom_call" | custom-call | tf_op jit(solution)/shard_map/store_results/pallas_call | solution.py:520
Async XLA Ops:
  67.5 0.6 copy-start
  68.1 0.6 copy-start.1
  68.8 0.6 copy-start.2
  69.4 0.6 copy-start.3

commit v4 on v3

--- a/solution.py
+++ b/solution.py
@@ -91,6 +91,8 @@
     f = lax.axis_index("fsdp")
     y, z = lax.div(d, nz), lax.rem(d, nz)
     i0, core = lax.div(f, 2), lax.rem(f, 2)
+    nx = ni // 2
+    x, yl = lax.div(i0, 2), lax.rem(i0, 2)
     mate = (d, 2 * i0 + 1 - core)
 
     def at_z(tz):
@@ -106,7 +108,7 @@
         ).start()
 
     started = []
-    own_w = rw.at[core, i0]
+    own_w = rw.at[core, yl, x]
     loads = [
         pltpu.make_async_copy(src, dst, in_sem.at[k])
         for k, (src, dst) in enumerate((
@@ -169,42 +171,39 @@
         send(rtag.at[z], rtag.at[z], sem.at[25], sem.at[26], at_z(tz))
 
     def send_w(k):
-        i = lax.rem(i0 + k, ni)
-        send(rw.at[core, i0], rw.at[core, i0], sem.at[6], sem.at[7], at_i(i))
+        send(own_w, own_w, sem.at[6], sem.at[7], at_i(2 * lax.rem(x + k, nx) + yl))
 
     for dy, dz in farthest_first(ny, nz):
         send_p(dy, dz)
     loop(1, nz, send_q)
-    loop(1, ni, send_w)
+    loop(1, nx, send_w)
     started += [
         (rtag.at[pl.ds(0, nz - 1)], sem.at[25]),
         (rp.at[pl.ds(0, ndp - 1)], sem.at[2]), (rq.at[pl.ds(0, nz - 1)], sem.at[4]),
-        (rw.at[0, pl.ds(0, ni - 1)], sem.at[6]),
     ]
+    if nx > 1:
+        started.append((rw.at[0, 0, pl.ds(0, nx - 1)], sem.at[6]))
 
     load_gain.wait()
     for k in range(gain_in.shape[0]):
         gain_row[0:1, 128 * k : 128 * (k + 1)] = gain_in[...].astype(F32)[k : k + 1, :]
 
-    landed(rw.at[core, pl.ds(0, ni - 1)], sem.at[7])
-    send(rw.at[core], rw.at[core], sem.at[10], sem.at[11], mate)
-    started.append((rw.at[0], sem.at[10]))
+    if nx > 1:
+        landed(rw.at[core, yl, pl.ds(0, nx - 1)], sem.at[7])
+    send(rw.at[core, yl], rw.at[core, yl], sem.at[10], sem.at[11], mate)
+    started.append((rw.at[0, 0], sem.at[10]))
     load_hid.wait()
 
-    def reduce_part(c, start):
-        def step(i, acc):
-            cols = pl.ds(pl.multiple_of((2 * i + c) * dw, 128), dw)
-            return acc + dot(rw[c, i][:, :dw], hid[:, cols], 1, 1)
-
-        return lax.fori_loop(0, ni, step, start)
-
-    reduced_t = reduce_part(core, jnp.zeros((rank, seq), F32))
-    landed(rw.at[1 - core], sem.at[11])
-    reduced_t = reduce_part(1 - core, reduced_t).astype(BF16)
-    for c in range(2):
-        for i in range(ni):
-            at = (2 * i + c) * uw
-            upf[:, at : at + uw] = rw[c, i][:, dw:]
+    def reduce_part(c, row, start):
+        def step(k, acc):
+            cols = pl.ds(pl.multiple_of((4 * k + 2 * row + c) * dw, 128), dw)
+            return acc + dot(rw[c, row, k][:, :dw], hid[:, cols], 1, 1)
+
+        return lax.fori_loop(0, nx, step, start, unroll=nx)
+
+    reduced_t = reduce_part(core, yl, jnp.zeros((rank, seq), F32))
+    landed(rw.at[1 - core, yl], sem.at[11])
+    reduced_t = reduce_part(1 - core, yl, reduced_t)
 
     landed(rq.at[pl.ds(0, nz - 1)], sem.at[5])
     landed(rtag.at[pl.ds(0, nz - 1)], sem.at[26])
@@ -225,19 +224,12 @@
     loop(1, nz, send_sc)
     started.append((rsc.at[pl.ds(0, nz - 1)], sem.at[27]))
 
-    load_res.wait()
-    cw = d_model // 4
-    reduced = reduced_t.astype(F32).T.astype(BF16)
-
-    def forward(j, squares):
-        cols = pl.ds(pl.multiple_of(j * cw, 128), cw)
-        part = res[:, cols].astype(F32) + 2.0 * dot(reduced, upf[:, cols])
-        normed[:, cols] = part
-        return squares + jnp.sum(part * part, axis=1, keepdims=True)
-
-    squares = lax.fori_loop(0, d_model // cw, forward, jnp.zeros((seq, 1), F32))
-    inv_root = 1.0 / jnp.sqrt(squares / d_model + EPS)
-    inv_row = as_row(inv_root)
+    send(rw.at[core, yl], rw.at[core, yl], sem.at[31], sem.at[32], at_i(2 * x + 1 - yl))
+    started.append((rw.at[0, 0], sem.at[31]))
+    landed(rw.at[core, 1 - yl], sem.at[32])
+    send(rw.at[core, 1 - yl], rw.at[core, 1 - yl], sem.at[33], sem.at[34], mate)
+    started.append((rw.at[0, 0], sem.at[33]))
+    reduced_t = reduce_part(core, 1 - yl, reduced_t)
 
     def coefficients(products, positive, hard_block):
         ids = lax.broadcasted_iota(jnp.int32, products.shape, 1)
@@ -269,6 +261,28 @@
     loop(1, nz, send_s)
     started.append((rs.at[pl.ds(0, nz - 1)], sem.at[8]))
 
+    landed(rw.at[1 - core, 1 - yl], sem.at[34])
+    reduced_t = reduce_part(1 - core, 1 - yl, reduced_t).astype(BF16)
+    for c in range(2):
+        for row in range(2):
+            for k in range(nx):
+                at = (4 * k + 2 * row + c) * uw
+                upf[:, at : at + uw] = rw[c, row, k][:, dw:]
+
+    load_res.wait()
+    cw = d_model // 4
+    reduced = reduced_t.astype(F32).T.astype(BF16)
+
+    def forward(j, squares):
+        cols = pl.ds(pl.multiple_of(j * cw, 128), cw)
+        part = res[:, cols].astype(F32) + 2.0 * dot(reduced, upf[:, cols])
+        normed[:, cols] = part
+        return squares + jnp.sum(part * part, axis=1, keepdims=True)
+
+    squares = lax.fori_loop(0, d_model // cw, forward, jnp.zeros((seq, 1), F32))
+    inv_root = 1.0 / jnp.sqrt(squares / d_model + EPS)
+    inv_row = as_row(inv_root)
+
     def normalize(j, acc):
         cols = pl.ds(pl.multiple_of(j * cw, 128), cw)
         part = normed[:, cols] * inv_root
@@ -360,8 +374,8 @@
 
     landed(rc.at[pl.ds(0, nz - 1)], sem.at[13])
     cmat = jnp.concatenate(split_rows(rc), axis=1)
-    for h in range(2):
-        qs[:, :, h * hw : (h + 1) * hw] = (SCALE * dot(cmat, pmat[h])).reshape(nz, 8, hw)
+    terms = [(SCALE * dot(cmat, pmat[h])).reshape(nz, 8, hw) for h in range(2)]
+    qs[...] = jnp.concatenate(terms, axis=1).astype(BF16)
     rqr[z] = qs[z]
 
     def send_qr(k):
@@ -374,11 +388,10 @@
     pgs[...] = jnp.concatenate(terms, axis=1).astype(BF16)
     rpg[d] = pgs[d]
 
-    def send_pg(k):
-        t = lax.rem(d + k, ndp)
+    for dy, dz in farthest_first(ny, nz):
+        t = lax.rem(y + dy, ny) * nz + lax.rem(z + dz, nz)
         send(pgs.at[t], rpg.at[d], sem.at[16], sem.at[17], (t, f))
 
-    loop(1, ndp, send_pg)
     started.append((rpg.at[pl.ds(0, ndp - 1)], sem.at[16]))
 
     @pl.when(is_owner)
@@ -393,7 +406,11 @@
 
 
     landed(rqr.at[pl.ds(0, nz - 1)], sem.at[15])
-    raw = jnp.concatenate([rqr[k] for k in range(nz)], axis=1)
+    pieces = []
+    for k in range(nz):
+        both = rqr[k].astype(F32)
+        pieces += [both[:8], both[8:]]
+    raw = jnp.concatenate(pieces, axis=1)
     qg_out[0] = tangent(unit_q[...], raw, len_q).astype(BF16)
 
     landed(rpg.at[pl.ds(0, ndp - 1)], sem.at[17])
@@ -495,11 +512,11 @@
             pltpu.VMEM((NZ, fb // 128, 128), F32),
             pltpu.VMEM((NZ, fb // 128, 128), F32),
             pltpu.VMEM((NZ, 16, pg // 2), BF16),
-            pltpu.VMEM((NZ, 8, fb), F32),
-            pltpu.VMEM((NZ, 8, fb), F32),
+            pltpu.VMEM((NZ, 16, hw), BF16),
+            pltpu.VMEM((NZ, 16, hw), BF16),
             pltpu.VMEM((ndp, 16, hw), BF16),
             pltpu.VMEM((ndp, 16, hw), BF16),
-            pltpu.VMEM((2, ni, rank, sw), BF16),
+            pltpu.VMEM((2, 2, ni // 2, rank, sw), BF16),
             pltpu.VMEM((rank, d_model), BF16),
             pltpu.VMEM((ni, rank, sw), BF16),
             pltpu.VMEM((ni, rank, sw), BF16),
@@ -508,7 +525,7 @@
             pltpu.VMEM((n_tiles, 8, 128), F32),
             pltpu.VMEM((ndp, 8, 128), F32),
             pltpu.VMEM((n_tiles, 8, 128), F32),
-            pltpu.SemaphoreType.DMA((31,)),
+            pltpu.SemaphoreType.DMA((35,)),
             pltpu.SemaphoreType.DMA((ni,)),
             pltpu.SemaphoreType.DMA((9,)),
         ],
@@ -523,8 +540,9 @@
         in_specs=[vmem] * 4,
         out_specs=(hbm,) * 4,
         scratch_shapes=[pltpu.SemaphoreType.DMA((4,))],
+        compiler_params=pltpu.CompilerParams(vmem_limit_bytes=2 * 1024 * 1024),
         name="store_results",
-    )(*results)
+    )(*(pltpu.with_memory_space_constraint(r, pltpu.VMEM) for r in results))
 
 
 def solution(mesh):

time: 71.8 us -> 64.2 us (0.89)
  Pallas kernels: 68.5 us -> 63.5 us
  local copies, waits for them, and re-layouts: 2.45 us -> 0 us
    pallas_call x1, Pallas kernels: 66.9 us -> 62.8 us  [per_device(): pl.pallas_call(functools.partial(kernel, ndp, nf), out_shape=(pltpu.VMEM(...]
    unnamed x8 -> x0, local copies, waits for them, and re-layouts: 2.45 us -> none
    pallas_call x1, Pallas kernels: 1.58 us -> 0.71 us  [per_device(): pl.pallas_call(store_kernel, out_shape=tuple((jax.ShapeDtypeStruct(r.shap...]
where the time goes in v4:
time: 64.2 us; the launch traced here: 64.1 us
  Pallas kernels  63.5 us (99%)
    pallas_call x1, Pallas kernels, per_device(): pl.pallas_call(functools.partial(kernel, ndp, nf), out_shape=(pltpu.VMEM(...  62.8 us

profile of v4, /device:TPU:2, one launch (start us, length us, event | category | flops | bytes accessed | tf_op | source)
XLA Modules:
  0.0 64.1 jit_solution(12383545993371062238)
XLA Ops:
  0.6 62.8 %contrastive_adapter.1 = (bf16[1,8,4096]{2,1,0:T(8,128)(2,1)S(1)}, bf16[1,8,4096]{2,1,0:T(8,128)(2,1)S(1)}, f32[16,896]{1,0:T(8,128)S(1)}, f32[16,256]{1,0:T(8,128)S(1)}) custom-call(bf16[1,8,4096]{2,1,0:T(8,128)(2,1)} %q_hbm.1, bf16[1,8,4096]{2,1,0:T(8,128)(2,1)} %p_hbm.1, s32[1,8]{1,0:T(1,128)} %pos_hbm.1, s32[1,8]{1,0:T(1,128)} %hard_hbm.1, ...), custom_call_target="tpu_custom_call" | custom-call | tf_op jit(solution)/shard_map/contrastive_adapter/pallas_call | solution.py:480
  63.4 0.7 %store_results.1 = (bf16[1,8,4096]{2,1,0:T(8,128)(2,1)}, bf16[1,8,4096]{2,1,0:T(8,128)(2,1)}, f32[16,896]{1,0:T(8,128)}, f32[16,256]{1,0:T(8,128)}) custom-call(bf16[1,8,4096]{2,1,0:T(8,128)(2,1)S(1)} %get-tuple-element.8.refs_0_, bf16[1,8,4096]{2,1,0:T(8,128)(2,1)S(1)} %get-tuple-element.9.refs_1_, f32[16,896]{1,0:T(8,128)S(1)} %get-tuple-element.10.refs_2_, ...), custom_call_target="tpu_custom_call" | custom-call | tf_op jit(solution)/shard_map/store_results/pallas_call | solution.py:537

commit v5 on v4

--- a/solution.py
+++ b/solution.py
@@ -50,6 +50,7 @@
 
 def split_rows(ref):
     wide = ref[...].astype(F32)
+    wide = wide.reshape((-1,) + wide.shape[-2:])
     n, _, w = wide.shape
     return [wide[:, 8 * h : 8 * h + 8, :].reshape(8 * n, w).astype(BF16) for h in (0, 1)]
 
@@ -69,8 +70,8 @@
     q_hbm, p_hbm, pos_hbm, hard_hbm, gain_hbm, down_hbm, up_hbm, res_hbm, hid_hbm,
     qg_out, pg_out, gd_out, gu_out,
     q_in, p_in, pos_in, hard_in, gain_in, hid, res, normed, unit_q, unit_p, gain_row,
-    eq, ep, rq, rp, pmat, qmat, ps, rs, rtag, rsc, qc, rqc, rc, qs, rqr, pgs, rpg,
-    rw, upf, sm, rmate, sa, ra, tiles, rb, rt,
+    eq, ep, rqa, rp, pmat, qmat, ps, rs, rtag, rsc, qc, rqc, rca, qs, rqr, pgs, rpg,
+    rw, upf, sm, rmate, sa, ra, ty, tz_sum,
     sem, msem, in_sem,
 ):
     nz = NZ
@@ -84,8 +85,6 @@
     hw = fb // 2
     seq = res.shape[0]
     pg = ndp * 8
-    n_tiles = tiles.shape[0]
-    nc = sw // 128
 
     d = lax.axis_index("dp")
     f = lax.axis_index("fsdp")
@@ -93,6 +92,7 @@
     i0, core = lax.div(f, 2), lax.rem(f, 2)
     nx = ni // 2
     x, yl = lax.div(i0, 2), lax.rem(i0, 2)
+    rq, rc = rqa.at[y], rca.at[y]
     mate = (d, 2 * i0 + 1 - core)
 
     def at_z(tz):
@@ -229,6 +229,15 @@
     landed(rw.at[core, 1 - yl], sem.at[32])
     send(rw.at[core, 1 - yl], rw.at[core, 1 - yl], sem.at[33], sem.at[34], mate)
     started.append((rw.at[0, 0], sem.at[33]))
+
+    def at_y(k):
+        return (lax.rem(y + k, ny) * nz + z, f)
+
+    def send_yq(k):
+        send(rqa.at[y], rqa.at[y], sem.at[35], sem.at[36], at_y(k))
+
+    loop(1, ny, send_yq)
+    started.append((rqa.at[pl.ds(0, ny - 1)], sem.at[35]))
     reduced_t = reduce_part(core, 1 - yl, reduced_t)
 
     def coefficients(products, positive, hard_block):
@@ -328,6 +337,16 @@
     loop(1, ni + 1, mate_step, unroll=ni)
     started.append((sm, sem.at[18]))
 
+    landed(rs.at[pl.ds(0, nz - 1)], sem.at[9])
+    coeffs = coefficients(jnp.sum(rs[...], axis=0), pos, hard)
+    rc[z] = stacked(coeffs).astype(BF16)
+
+    def send_c(k):
+        send(rc.at[z], rc.at[z], sem.at[12], sem.at[13], at_z(lax.rem(z + k, nz)))
+
+    loop(1, nz, send_c)
+    started.append((rc.at[pl.ds(0, nz - 1)], sem.at[12]))
+
     def own_terms(i, out_ref, out_at):
         down_term, up_term = terms_of(i, core)
         landed(rmate.at[i], msem.at[i])
@@ -344,34 +363,6 @@
     started.append((sa.at[pl.ds(0, ni - 1)], sem.at[19]))
     own_terms(i0, ra, i0)
 
-    landed(rs.at[pl.ds(0, nz - 1)], sem.at[9])
-    coeffs = coefficients(jnp.sum(rs[...], axis=0), pos, hard)
-    rc[z] = stacked(coeffs).astype(BF16)
-
-    def send_c(k):
-        send(rc.at[z], rc.at[z], sem.at[12], sem.at[13], at_z(lax.rem(z + k, nz)))
-
-    loop(1, nz, send_c)
-    started.append((rc.at[pl.ds(0, nz - 1)], sem.at[12]))
-
-    landed(ra.at[pl.ds(0, ni - 1)], sem.at[20])
-    total = jnp.sum(ra[...].astype(F32), axis=0)
-    for k in range(n_tiles):
-        h, c = k // nc, k % nc
-        tiles[k] = total[8 * h : 8 * h + 8, 128 * c : 128 * c + 128]
-
-    own_tile = lax.div(d * n_tiles + ndp - 1, ndp)
-    is_owner = (lax.div(own_tile * ndp, n_tiles) == d) & (own_tile < n_tiles)
-
-    def send_tile(k):
-        t = lax.div(k * ndp, n_tiles)
-
-        @pl.when(t != d)
-        def _():
-            send(tiles.at[k], rb.at[d], sem.at[21], sem.at[22], (t, f))
-
-    loop(0, n_tiles, send_tile)
-
     landed(rc.at[pl.ds(0, nz - 1)], sem.at[13])
     cmat = jnp.concatenate(split_rows(rc), axis=1)
     terms = [(SCALE * dot(cmat, pmat[h])).reshape(nz, 8, hw) for h in range(2)]
@@ -384,71 +375,63 @@
 
     loop(1, nz, send_qr)
     started.append((rqr.at[pl.ds(0, nz - 1)], sem.at[14]))
-    terms = [(SCALE * dot(cmat, qmat[h], 0, 0)).reshape(ndp, 8, hw) for h in range(2)]
+
+    def send_yc(k):
+        send(rca.at[y], rca.at[y], sem.at[37], sem.at[38], at_y(k))
+
+    loop(1, ny, send_yc)
+    started.append((rca.at[pl.ds(0, ny - 1)], sem.at[37]))
+
+    landed(ra.at[pl.ds(0, ni - 1)], sem.at[20])
+    ty[y] = jnp.sum(ra[...].astype(F32), axis=0).astype(BF16)
+
+    def send_ty(k):
+        send(ty.at[y], ty.at[y], sem.at[21], sem.at[22], (lax.rem(y + k, ny) * nz + z, f))
+
+    loop(1, ny, send_ty, unroll=ny - 1)
+    started.append((ty.at[pl.ds(0, ny - 1)], sem.at[21]))
+
+    landed(rqa.at[pl.ds(0, ny - 1)], sem.at[36])
+    landed(rca.at[pl.ds(0, ny - 1)], sem.at[38])
+    call = jnp.concatenate(split_rows(rca), axis=1)
+    terms = [(SCALE * dot(call, half, 0, 0)).reshape(ndp, 8, hw) for half in split_rows(rqa)]
     pgs[...] = jnp.concatenate(terms, axis=1).astype(BF16)
-    rpg[d] = pgs[d]
-
-    for dy, dz in farthest_first(ny, nz):
-        t = lax.rem(y + dy, ny) * nz + lax.rem(z + dz, nz)
-        send(pgs.at[t], rpg.at[d], sem.at[16], sem.at[17], (t, f))
-
-    started.append((rpg.at[pl.ds(0, ndp - 1)], sem.at[16]))
-
-    @pl.when(is_owner)
-    def _():
-        rb[d] = tiles[own_tile]
-        landed(rb.at[pl.ds(0, ndp - 1)], sem.at[22])
-        rt[own_tile] = jnp.sum(rb[...], axis=0)
-
-        for dy, dz in farthest_first(ny, nz):
-            t = lax.rem(y + dy, ny) * nz + lax.rem(z + dz, nz)
-            send(rt.at[own_tile], rt.at[own_tile], sem.at[23], sem.at[24], (t, f))
-
+    rpg[z] = pgs[d]
+
+    def send_pg(k):
+        tz = lax.rem(z + k, nz)
+        send(pgs.at[y * nz + tz], rpg.at[z], sem.at[16], sem.at[17], at_z(tz))
+
+    loop(1, nz, send_pg)
+    started.append((rpg.at[pl.ds(0, nz - 1)], sem.at[16]))
+
+    landed(ty.at[pl.ds(0, ny - 1)], sem.at[22])
+    tz_sum[z] = jnp.sum(ty[...].astype(F32), axis=0).astype(BF16)
+
+    def send_tz(k):
+        send(tz_sum.at[z], tz_sum.at[z], sem.at[23], sem.at[24], at_z(lax.rem(z + nz // 2 + k, nz)))
+
+    for k in sorted(range(nz), key=lambda k: min((nz // 2 + k) % nz, nz - (nz // 2 + k) % nz), reverse=True)[:-1]:
+        send_tz(k)
+    started.append((tz_sum.at[pl.ds(0, nz - 1)], sem.at[23]))
+
+    def unfolded(ref):
+        wide = ref[...].astype(F32)
+        return jnp.concatenate([wide[k, 8 * h : 8 * h + 8] for k in range(nz) for h in range(2)], axis=1)
 
     landed(rqr.at[pl.ds(0, nz - 1)], sem.at[15])
-    pieces = []
-    for k in range(nz):
-        both = rqr[k].astype(F32)
-        pieces += [both[:8], both[8:]]
-    raw = jnp.concatenate(pieces, axis=1)
-    qg_out[0] = tangent(unit_q[...], raw, len_q).astype(BF16)
-
-    landed(rpg.at[pl.ds(0, ndp - 1)], sem.at[17])
-    pieces = []
-    for k in range(nz):
-        both = rpg[k].astype(F32)
-        for a in range(1, ny):
-            both = both + rpg[a * nz + k].astype(F32)
-        pieces += [both[:8], both[8:]]
-    pg_out[0] = tangent(unit_p[...], jnp.concatenate(pieces, axis=1), len_p).astype(BF16)
-
-    @pl.when(is_owner)
-    def _():
-        landed(rt.at[pl.ds(0, n_tiles - 1)], sem.at[24])
-
-    @pl.when(jnp.logical_not(is_owner))
-    def _():
-        landed(rt, sem.at[24])
-
-    for k in range(n_tiles):
-        h, c = k // nc, k % nc
-        if c < dw // 128:
-            gd_out[8 * h : 8 * h + 8, 128 * c : 128 * c + 128] = rt[k]
-        else:
-            at = 128 * c - dw
-            gu_out[8 * h : 8 * h + 8, at : at + 128] = rt[k]
+    qg_out[0] = tangent(unit_q[...], unfolded(rqr), len_q).astype(BF16)
+
+    landed(rpg.at[pl.ds(0, nz - 1)], sem.at[17])
+    pg_out[0] = tangent(unit_p[...], unfolded(rpg), len_p).astype(BF16)
+
+    landed(tz_sum.at[pl.ds(0, nz - 1)], sem.at[24])
+    total = jnp.sum(tz_sum[...].astype(F32), axis=0)
+    gd_out[...] = total[:, :dw]
+    gu_out[...] = total[:, dw:]
 
     for ref, left in started:
         landed(ref, left)
-
-    @pl.when(is_owner)
-    def _():
-        landed(tiles.at[pl.ds(0, n_tiles - 1)], sem.at[21])
-        landed(rb.at[pl.ds(0, ndp - 1)], sem.at[23])
-
-    @pl.when(jnp.logical_not(is_owner))
-    def _():
-        landed(tiles, sem.at[21])
 
 
 def store_kernel(*refs):
@@ -470,7 +453,6 @@
     fb = d_model // NZ
     hw = fb // 2
     pg = ndp * 8
-    n_tiles = (rank // 8) * (sw // 128)
     hbm = pl.BlockSpec(memory_space=pltpu.HBM)
     vmem = pl.BlockSpec(memory_space=pltpu.VMEM)
     operands = (
@@ -501,7 +483,7 @@
             pltpu.VMEM((1, d_model), F32),
             pltpu.VMEM((NZ, 16, hw), BF16),
             pltpu.VMEM((NZ, 16, hw), BF16),
-            pltpu.VMEM((NZ, 16, hw), BF16),
+            pltpu.VMEM((ndp // NZ, NZ, 16, hw), BF16),
             pltpu.VMEM((ndp, 16, hw), BF16),
             pltpu.VMEM((2, pg, hw), BF16),
             pltpu.VMEM((2, 8 * NZ, hw), BF16),
@@ -511,21 +493,20 @@
             pltpu.VMEM((NZ, NZ, pg), F32),
             pltpu.VMEM((NZ, fb // 128, 128), F32),
             pltpu.VMEM((NZ, fb // 128, 128), F32),
-            pltpu.VMEM((NZ, 16, pg // 2), BF16),
+            pltpu.VMEM((ndp // NZ, NZ, 16, pg // 2), BF16),
             pltpu.VMEM((NZ, 16, hw), BF16),
             pltpu.VMEM((NZ, 16, hw), BF16),
             pltpu.VMEM((ndp, 16, hw), BF16),
-            pltpu.VMEM((ndp, 16, hw), BF16),
+            pltpu.VMEM((NZ, 16, hw), BF16),
             pltpu.VMEM((2, 2, ni // 2, rank, sw), BF16),
             pltpu.VMEM((rank, d_model), BF16),
             pltpu.VMEM((ni, rank, sw), BF16),
             pltpu.VMEM((ni, rank, sw), BF16),
             pltpu.VMEM((ni, rank, sw), BF16),
             pltpu.VMEM((ni, rank, sw), BF16),
-            pltpu.VMEM((n_tiles, 8, 128), F32),
-            pltpu.VMEM((ndp, 8, 128), F32),
-            pltpu.VMEM((n_tiles, 8, 128), F32),
-            pltpu.SemaphoreType.DMA((35,)),
+            pltpu.VMEM((ndp // NZ, rank, sw), BF16),
+            pltpu.VMEM((NZ, rank, sw), BF16),
+            pltpu.SemaphoreType.DMA((39,)),
             pltpu.SemaphoreType.DMA((ni,)),
             pltpu.SemaphoreType.DMA((9,)),
         ],

time: 64.2 us -> 62.4 us (0.972)
  the two profiles are of different devices: /device:TPU:2 before, /device:TPU:1 now
where the time goes in v5:
time: 62.4 us; the launch traced here: 62.2 us
  Pallas kernels  61.6 us (99%)
  between operations  0.64 us (1%)
    pallas_call x1, Pallas kernels, per_device(): pl.pallas_call(functools.partial(kernel, ndp, nf), out_shape=(pltpu.VMEM(...  60.9 us

profile of v5, /device:TPU:1, one launch (start us, length us, event | category | flops | bytes accessed | tf_op | source)
XLA Modules:
  0.0 62.2 jit_solution(3293575098318101716)
XLA Ops:
  0.6 60.9 %contrastive_adapter.1 = (bf16[1,8,4096]{2,1,0:T(8,128)(2,1)S(1)}, bf16[1,8,4096]{2,1,0:T(8,128)(2,1)S(1)}, f32[16,896]{1,0:T(8,128)S(1)}, f32[16,256]{1,0:T(8,128)S(1)}) custom-call(bf16[1,8,4096]{2,1,0:T(8,128)(2,1)} %q_hbm.1, bf16[1,8,4096]{2,1,0:T(8,128)(2,1)} %p_hbm.1, s32[1,8]{1,0:T(1,128)} %pos_hbm.1, s32[1,8]{1,0:T(1,128)} %hard_hbm.1, ...), custom_call_target="tpu_custom_call" | custom-call | tf_op jit(solution)/shard_map/contrastive_adapter/pallas_call | solution.py:462
  61.5 0.7 %store_results.1 = (bf16[1,8,4096]{2,1,0:T(8,128)(2,1)}, bf16[1,8,4096]{2,1,0:T(8,128)(2,1)}, f32[16,896]{1,0:T(8,128)}, f32[16,256]{1,0:T(8,128)}) custom-call(bf16[1,8,4096]{2,1,0:T(8,128)(2,1)S(1)} %get-tuple-element.8.refs_0_, bf16[1,8,4096]{2,1,0:T(8,128)(2,1)S(1)} %get-tuple-element.9.refs_1_, f32[16,896]{1,0:T(8,128)S(1)} %get-tuple-element.10.refs_2_, ...), custom_call_target="tpu_custom_call" | custom-call | tf_op jit(solution)/shard_map/store_results/pallas_call | solution.py:518

commit v6 on v5

--- a/solution.py
+++ b/solution.py
@@ -65,12 +65,16 @@
     return sorted(offsets, key=lambda o: -(2 * min(o[0], ny - o[0]) + min(o[1], nz - o[1])))
 
 
+def far_z(nz):
+    return sorted(range(1, nz), key=lambda k: -min(k, nz - k))
+
+
 def kernel(
     ndp, nf,
     q_hbm, p_hbm, pos_hbm, hard_hbm, gain_hbm, down_hbm, up_hbm, res_hbm, hid_hbm,
     qg_out, pg_out, gd_out, gu_out,
     q_in, p_in, pos_in, hard_in, gain_in, hid, res, normed, unit_q, unit_p, gain_row,
-    eq, ep, rqa, rp, pmat, qmat, ps, rs, rtag, rsc, qc, rqc, rca, qs, rqr, pgs, rpg,
+    eq, ep, rqa, rp, pmat, qmat, ps, rs, rtag, rsc, qc, rqc, rc, cy, rcy, qs, rqr, pgs, rpg,
     rw, upf, sm, rmate, sa, ra, ty, tz_sum,
     sem, msem, in_sem,
 ):
@@ -85,6 +89,7 @@
     hw = fb // 2
     seq = res.shape[0]
     pg = ndp * 8
+    pb = pg // ny
 
     d = lax.axis_index("dp")
     f = lax.axis_index("fsdp")
@@ -92,7 +97,7 @@
     i0, core = lax.div(f, 2), lax.rem(f, 2)
     nx = ni // 2
     x, yl = lax.div(i0, 2), lax.rem(i0, 2)
-    rq, rc = rqa.at[y], rca.at[y]
+    rq = rqa.at[y]
     mate = (d, 2 * i0 + 1 - core)
 
     def at_z(tz):
@@ -175,7 +180,8 @@
 
     for dy, dz in farthest_first(ny, nz):
         send_p(dy, dz)
-    loop(1, nz, send_q)
+    for k in far_z(nz):
+        send_q(k)
     loop(1, nx, send_w)
     started += [
         (rtag.at[pl.ds(0, nz - 1)], sem.at[25]),
@@ -221,7 +227,8 @@
     def send_sc(k):
         send(rsc.at[z], rsc.at[z], sem.at[27], sem.at[28], at_z(lax.rem(z + k, nz)))
 
-    loop(1, nz, send_sc)
+    for k in far_z(nz):
+        send_sc(k)
     started.append((rsc.at[pl.ds(0, nz - 1)], sem.at[27]))
 
     send(rw.at[core, yl], rw.at[core, yl], sem.at[31], sem.at[32], at_i(2 * x + 1 - yl))
@@ -260,14 +267,16 @@
         tz = lax.rem(z + k, nz)
         send(qc.at[tz], rqc.at[z], sem.at[29], sem.at[30], at_z(tz))
 
-    loop(1, nz, send_qc)
+    for k in far_z(nz):
+        send_qc(k)
     started.append((rqc.at[pl.ds(0, nz - 1)], sem.at[29]))
 
     def send_s(k):
         tz = lax.rem(z + k, nz)
         send(ps.at[tz], rs.at[z], sem.at[8], sem.at[9], at_z(tz))
 
-    loop(1, nz, send_s)
+    for k in far_z(nz):
+        send_s(k)
     started.append((rs.at[pl.ds(0, nz - 1)], sem.at[8]))
 
     landed(rw.at[1 - core, 1 - yl], sem.at[34])
@@ -331,10 +340,12 @@
         sm[i, :, dw:] = up_term.astype(BF16)
         send(sm.at[i], rmate.at[i], sem.at[18], msem.at[i], mate)
 
-    def mate_step(k):
-        for_mate(lax.rem(i0 + k, ni))
-
-    loop(1, ni + 1, mate_step, unroll=ni)
+    def owner_of(dx, dyl):
+        return 2 * lax.rem(x + dx, nx) + lax.rem(yl + dyl, 2)
+
+    order = sorted(((dx, dyl) for dx in range(nx) for dyl in range(2)), key=lambda o: -(min(o[0], nx - o[0]) + o[1]))
+    for dx, dyl in order:
+        for_mate(owner_of(dx, dyl))
     started.append((sm, sem.at[18]))
 
     landed(rs.at[pl.ds(0, nz - 1)], sem.at[9])
@@ -344,7 +355,8 @@
     def send_c(k):
         send(rc.at[z], rc.at[z], sem.at[12], sem.at[13], at_z(lax.rem(z + k, nz)))
 
-    loop(1, nz, send_c)
+    for k in far_z(nz):
+        send_c(k)
     started.append((rc.at[pl.ds(0, nz - 1)], sem.at[12]))
 
     def own_terms(i, out_ref, out_at):
@@ -354,17 +366,28 @@
         out_ref[out_at, :, :dw] = (down_term + other[:, :dw]).astype(BF16)
         out_ref[out_at, :, dw:] = (up_term + other[:, dw:]).astype(BF16)
 
-    def own_step(k):
-        i = lax.rem(i0 + k, ni)
+    for dx, dyl in order[:-1]:
+        i = owner_of(dx, dyl)
         own_terms(i, sa, i)
         send(sa.at[i], ra.at[i0], sem.at[19], sem.at[20], at_i(i))
-
-    loop(1, ni, own_step, unroll=ni - 1)
     started.append((sa.at[pl.ds(0, ni - 1)], sem.at[19]))
     own_terms(i0, ra, i0)
 
     landed(rc.at[pl.ds(0, nz - 1)], sem.at[13])
     cmat = jnp.concatenate(split_rows(rc), axis=1)
+
+    wide_c = cmat.astype(F32)
+    half_rows = 4 * nz
+    for k in range(ny):
+        block = wide_c[:, pb * k : pb * k + pb]
+        cy[k] = jnp.concatenate([block[:half_rows], block[half_rows:]], axis=1).astype(BF16)
+    rcy[y] = cy[y]
+
+    def send_yc(k):
+        send(cy.at[lax.rem(y + k, ny)], rcy.at[y], sem.at[37], sem.at[38], at_y(k))
+
+    loop(1, ny, send_yc)
+    started.append((rcy.at[pl.ds(0, ny - 1)], sem.at[37]))
     terms = [(SCALE * dot(cmat, pmat[h])).reshape(nz, 8, hw) for h in range(2)]
     qs[...] = jnp.concatenate(terms, axis=1).astype(BF16)
     rqr[z] = qs[z]
@@ -373,14 +396,9 @@
         tz = lax.rem(z + k, nz)
         send(qs.at[tz], rqr.at[z], sem.at[14], sem.at[15], at_z(tz))
 
-    loop(1, nz, send_qr)
+    for k in far_z(nz):
+        send_qr(k)
     started.append((rqr.at[pl.ds(0, nz - 1)], sem.at[14]))
-
-    def send_yc(k):
-        send(rca.at[y], rca.at[y], sem.at[37], sem.at[38], at_y(k))
-
-    loop(1, ny, send_yc)
-    started.append((rca.at[pl.ds(0, ny - 1)], sem.at[37]))
 
     landed(ra.at[pl.ds(0, ni - 1)], sem.at[20])
     ty[y] = jnp.sum(ra[...].astype(F32), axis=0).astype(BF16)
@@ -392,26 +410,29 @@
     started.append((ty.at[pl.ds(0, ny - 1)], sem.at[21]))
 
     landed(rqa.at[pl.ds(0, ny - 1)], sem.at[36])
-    landed(rca.at[pl.ds(0, ny - 1)], sem.at[38])
-    call = jnp.concatenate(split_rows(rca), axis=1)
-    terms = [(SCALE * dot(call, half, 0, 0)).reshape(ndp, 8, hw) for half in split_rows(rqa)]
+    landed(rcy.at[pl.ds(0, ny - 1)], sem.at[38])
+    wide_c = rcy[...].astype(F32)
+    blocks_c = [wide_c[k][:, pb * h : pb * h + pb] for k in range(ny) for h in range(2)]
+    call = jnp.concatenate(blocks_c, axis=0).astype(BF16)
+    terms = [(SCALE * dot(call, half, 0, 0)).reshape(nz, 8, hw) for half in split_rows(rqa)]
     pgs[...] = jnp.concatenate(terms, axis=1).astype(BF16)
-    rpg[z] = pgs[d]
+    rpg[z] = pgs[z]
 
     def send_pg(k):
         tz = lax.rem(z + k, nz)
-        send(pgs.at[y * nz + tz], rpg.at[z], sem.at[16], sem.at[17], at_z(tz))
-
-    loop(1, nz, send_pg)
+        send(pgs.at[tz], rpg.at[z], sem.at[16], sem.at[17], at_z(tz))
+
+    for k in far_z(nz):
+        send_pg(k)
     started.append((rpg.at[pl.ds(0, nz - 1)], sem.at[16]))
 
     landed(ty.at[pl.ds(0, ny - 1)], sem.at[22])
     tz_sum[z] = jnp.sum(ty[...].astype(F32), axis=0).astype(BF16)
 
     def send_tz(k):
-        send(tz_sum.at[z], tz_sum.at[z], sem.at[23], sem.at[24], at_z(lax.rem(z + nz // 2 + k, nz)))
-
-    for k in sorted(range(nz), key=lambda k: min((nz // 2 + k) % nz, nz - (nz // 2 + k) % nz), reverse=True)[:-1]:
+        send(tz_sum.at[z], tz_sum.at[z], sem.at[23], sem.at[24], at_z(lax.rem(z + k, nz)))
+
+    for k in far_z(nz):
         send_tz(k)
     started.append((tz_sum.at[pl.ds(0, nz - 1)], sem.at[23]))
 
@@ -493,10 +514,12 @@
             pltpu.VMEM((NZ, NZ, pg), F32),
             pltpu.VMEM((NZ, fb // 128, 128), F32),
             pltpu.VMEM((NZ, fb // 128, 128), F32),
-            pltpu.VMEM((ndp // NZ, NZ, 16, pg // 2), BF16),
+            pltpu.VMEM((NZ, 16, pg // 2), BF16),
+            pltpu.VMEM((ndp // NZ, 4 * NZ, 2 * pg // (ndp // NZ)), BF16),
+            pltpu.VMEM((ndp // NZ, 4 * NZ, 2 * pg // (ndp // NZ)), BF16),
             pltpu.VMEM((NZ, 16, hw), BF16),
             pltpu.VMEM((NZ, 16, hw), BF16),
-            pltpu.VMEM((ndp, 16, hw), BF16),
+            pltpu.VMEM((NZ, 16, hw), BF16),
             pltpu.VMEM((NZ, 16, hw), BF16),
             pltpu.VMEM((2, 2, ni // 2, rank, sw), BF16),
             pltpu.VMEM((rank, d_model), BF16),

time: 62.4 us -> 61.4 us (0.984)
  the two profiles are of different devices: /device:TPU:1 before, /device:TPU:16 now
where the time goes in v6:
time: 61.4 us; the launch traced here: 61.3 us
  Pallas kernels  60.7 us (99%)
  between operations  0.64 us (1%)
    pallas_call x1, Pallas kernels, per_device(): pl.pallas_call(functools.partial(kernel, ndp, nf), out_shape=(pltpu.VMEM(...  59.9 us

profile of v6, /device:TPU:16, one launch (start us, length us, event | category | flops | bytes accessed | tf_op | source)
XLA Modules:
  0.0 61.3 jit_solution(11817401240119196911)
XLA Ops:
  0.6 59.9 %contrastive_adapter.1 = (bf16[1,8,4096]{2,1,0:T(8,128)(2,1)S(1)}, bf16[1,8,4096]{2,1,0:T(8,128)(2,1)S(1)}, f32[16,896]{1,0:T(8,128)S(1)}, f32[16,256]{1,0:T(8,128)S(1)}) custom-call(bf16[1,8,4096]{2,1,0:T(8,128)(2,1)} %q_hbm.1, bf16[1,8,4096]{2,1,0:T(8,128)(2,1)} %p_hbm.1, s32[1,8]{1,0:T(1,128)} %pos_hbm.1, s32[1,8]{1,0:T(1,128)} %hard_hbm.1, ...), custom_call_target="tpu_custom_call" | custom-call | tf_op jit(solution)/shard_map/contrastive_adapter/pallas_call | solution.py:483
  60.6 0.7 %store_results.1 = (bf16[1,8,4096]{2,1,0:T(8,128)(2,1)}, bf16[1,8,4096]{2,1,0:T(8,128)(2,1)}, f32[16,896]{1,0:T(8,128)}, f32[16,256]{1,0:T(8,128)}) custom-call(bf16[1,8,4096]{2,1,0:T(8,128)(2,1)S(1)} %get-tuple-element.8.refs_0_, bf16[1,8,4096]{2,1,0:T(8,128)(2,1)S(1)} %get-tuple-element.9.refs_1_, f32[16,896]{1,0:T(8,128)S(1)} %get-tuple-element.10.refs_2_, ...), custom_call_target="tpu_custom_call" | custom-call | tf_op jit(solution)/shard_map/store_results/pallas_call | solution.py:541
